TPU v7x, 32 devices: a whole 2x2x4 slice. The times are simulated.
32 devices in a mesh: groups: 2 (over y), ep: 4 (over z), fsdp: 4 (over x, core).
Axes of the slice: x: 2, y: 2, z: 4, core: 2. Of those that a mesh axis runs over, the one named last changes fastest.
Arguments:
- layer_in: bfloat16 [4096, 1536], P(('groups', 'ep', 'fsdp')), parts along dimension 0, may hold values from -24 to 24
- attn_out: bfloat16 [4096, 1536], P(('groups', 'ep', 'fsdp')), parts along dimension 0, may hold values from -6 to 6
- norm_gain: float32 [1536], replicated, may hold values from 0.1 to 1.9
- expert_ids: int32 [4096, 2], P(('groups', 'ep', 'fsdp')), parts along dimension 0, may hold values from 0 to 1, as said below
- gate_weights: float32 [4096, 2], P(('groups', 'ep', 'fsdp')), parts along dimension 0, may hold values from 0.1 to 1
- w_gate_up: bfloat16 [4, 1536, 1536], P('ep', None, 'fsdp'), may hold values from -0.15625 to 0.15625
- w_down: bfloat16 [4, 768, 1536], P('ep', None, 'fsdp'), may hold values from -0.15625 to 0.15625
Outputs:
- layer_out: bfloat16 [4096, 1536], P(('groups', 'ep', 'fsdp')), parts along dimension 0
- similarity: float32 [4096], P(('groups', 'ep', 'fsdp')), parts along dimension 0
There are 2 independent parts, one for each index of `groups`. A program takes and returns all parts, laid end to end along the dimension named above; an argument that names none is the same for every part. Nothing has to cross between parts.
Inputs may be any that keep to these rules, and one draw needn't show every extreme that they name: `expert_ids`: the 2 ids of a row differ. In each aligned block of 128 rows (the tokens of one device) no expert is named more than 128 times; one expert, the same in every block, is named exactly 128 times in each block.
All inputs are finite; a program needn't handle non-finite values.
Results may differ from a plain program's by a relative error of at most 0.004.
Values may be sent and summed in bfloat16 or wider, within the bound.
No kernel may reach another device: no remote copies, remote signals or barrier semaphores. Data moves between devices by JAX's collectives and lax.ppermute only.
A program may use at most 64 MiB of HBM per device.

v0:
```python
import jax
import jax.numpy as jnp
from jax import lax
from jax.sharding import PartitionSpec as P

norm_eps = 1e-05
cos_eps = 1e-06
glu_alpha = 1.702


def swapped(value, axis, bit):
    mask = 2**bit
    pairs = [(source, source ^ mask) for source in range(lax.axis_size(axis))]
    return lax.ppermute(value, axis, pairs)


def activate(projected, half_hidden):
    gate_part = projected[:, :half_hidden]
    up_part = projected[:, half_hidden:]
    return (gate_part * jax.nn.sigmoid(glu_alpha * gate_part) * (up_part + 1.0)).astype(
        jnp.bfloat16
    )


def shards(layer_in, attn_out, norm_gain, expert_ids, gate_weights, w_gate_up, w_down):
    tokens, features = layer_in.shape
    routes = expert_ids.shape[1]
    devices_ep = lax.axis_size("ep")
    experts = devices_ep // 2
    capacity = min(tokens, 2 * tokens * routes // experts)
    half_cap = capacity // 2
    hidden = w_gate_up.shape[2] * lax.axis_size("fsdp")
    half_hidden = hidden // 2
    inputs = layer_in.astype(jnp.float32)
    residual = inputs + attn_out.astype(jnp.float32)
    mean_square = jnp.mean(residual * residual, axis=-1, keepdims=True)
    normed = (residual * lax.rsqrt(mean_square + norm_eps) * norm_gain[None, :]).astype(
        jnp.bfloat16
    )
    flat_ids = expert_ids.reshape(-1)
    onehot = (flat_ids[:, None] == jnp.arange(experts, dtype=jnp.int32)[None, :]).astype(jnp.int32)
    earlier = jnp.cumsum(onehot, axis=0) - onehot
    slot_index = jnp.sum(earlier * onehot, axis=1)
    target = flat_ids * capacity + slot_index
    outgoing = (
        jnp.zeros((experts * capacity, features), jnp.bfloat16)
        .at[target]
        .set(jnp.repeat(normed, routes, axis=0))
    )
    outgoing = outgoing.reshape(experts, capacity, features)
    parity = lax.axis_index("ep") % 2
    doubled = jnp.repeat(outgoing, 2, axis=0)
    arrived = lax.all_to_all(doubled, "ep", split_axis=0, concat_axis=0, tiled=True)
    slot_rows = arrived.reshape(devices_ep * capacity, features)
    full_up, full_down = (
        lax.all_gather(w_gate_up, "fsdp", axis=2, tiled=True),
        lax.all_gather(w_down, "fsdp", axis=2, tiled=True),
    )
    projected = jnp.dot(slot_rows, full_up[0], preferred_element_type=jnp.float32)
    activated = activate(projected, half_hidden)
    partial_value = jnp.dot(activated, full_down[0], preferred_element_type=jnp.float32)
    partial_value = partial_value.reshape(devices_ep, capacity, features)
    kept_half = lax.dynamic_slice_in_dim(partial_value, parity * half_cap, half_cap, 1)
    sent_half = lax.dynamic_slice_in_dim(partial_value, (1 - parity) * half_cap, half_cap, 1)
    received = swapped(sent_half.astype(jnp.bfloat16), "ep", 0).astype(sent_half.dtype)
    summed = (kept_half + received).astype(jnp.bfloat16)
    returned = lax.all_to_all(summed, "ep", split_axis=0, concat_axis=0, tiled=True)
    returned = returned.reshape(experts * capacity, features)
    per_route = returned[target].reshape(tokens, routes, features).astype(jnp.float32)
    mixture = jnp.sum(gate_weights[:, :, None] * per_route, axis=1)
    updated = residual + mixture
    inner = jnp.sum(inputs * updated, axis=-1)
    similarity = (
        inner
        * lax.rsqrt(jnp.sum(inputs * inputs, axis=-1) + cos_eps)
        * lax.rsqrt(jnp.sum(updated * updated, axis=-1) + cos_eps)
    )
    return (updated.astype(jnp.bfloat16), similarity)


def solution(mesh):
    placed = (
        P(("groups", "ep", "fsdp"), None),
        P(("groups", "ep", "fsdp"), None),
        P(),
        P(("groups", "ep", "fsdp"), None),
        P(("groups", "ep", "fsdp"), None),
        P("ep", None, "fsdp"),
        P("ep", None, "fsdp"),
    )
    return jax.shard_map(
        shards,
        mesh=mesh,
        in_specs=placed,
        out_specs=(P(("groups", "ep", "fsdp"), None), P(("groups", "ep", "fsdp"))),
        check_vma=False,
    )
```

profile of v0, /device:TPU:0, one launch (start us, length us, event | category | flops | bytes accessed | tf_op | source)
XLA Modules:
  0.0 139.7 jit_solution(7591855212401234453)
XLA Ops:
  7.2 0.7 all-gather.3.cloned.1.call-update
  8.0 0.7 all-gather.5.cloned.1.call-update
  8.7 0.1 copy.12
  8.8 0.1 eq.31
  9.0 0.1 eq.27
  9.2 0.1 mul.82
  9.4 0.6 reduce-window.6
  10.0 0.2 slice_reduce_fusion
  10.2 0.2 reduce-window.9
  10.5 0.2 multiply_reduce_fusion.2
  10.7 0.2 multiply_convert_fusion
  10.9 0.4 broadcast_in_dim.7
  11.3 0.3 reshape.99
  11.6 2.0 %scatter_custom_fusion = bf16[256,1536]{1,0:T(8,128)(2,1)S(1)} fusion(s32[256]{0:T(256)S(1)} %bitcast.39, bf16[256,1536]{1,0:T(8,128)(2,1)S(1)} %reshape.99, bf16[]{:T(256)} %constant.15.clone.1), kind=kCustom, calls=%fused_computation.21 | custom fusion | bytes 786434 | tf_op jit(solution)/shard_map/scatter | solution.py:48
  13.6 1.3 broadcast_in_dim.8
  15.0 6.3 %all-to-all-start = ((bf16[4,128,1536]{2,1,0:T(8,128)(2,1)}), bf16[4,128,1536]{2,1,0:T(8,128)(2,1)S(1)}, u32[]{:S(2)}, u32[]{:S(2)}) async-start(bf16[4,128,1536]{2,1,0:T(8,128)(2,1)} %bitcast.4), calls=%async_computation | async-start | bytes 3145728 | tf_op jit(solution)/shard_map/all_to_all | solution.py:53
  21.3 37.0 %all-to-all-done = bf16[4,128,1536]{2,1,0:T(8,128)(2,1)S(1)} async-done(((bf16[4,128,1536]{2,1,0:T(8,128)(2,1)}), bf16[4,128,1536]{2,1,0:T(8,128)(2,1)S(1)}, u32[]{:S(2)}, u32[]{:S(2)}) %all-to-all-start) | async-done | bytes 1572896 | tf_op jit(solution)/shard_map/all_to_all | solution.py:53
  58.2 4.8 %fusion = f32[512,1536]{1,0:T(8,128)S(1)} fusion(bf16[512,1536]{1,0:T(8,128)(2,1)S(1)} %bitcast.37, bf16[1,1536,1536]{2,1,0:T(8,128)(2,1)} %all-gather.3.cloned.1.call-done), kind=kOutput, calls=%fused_computation.2 | convolution fusion | flops 2415919104 | bytes 9437184 | tf_op jit(solution)/shard_map/dot_general | solution.py:59
  63.0 0.5 fusion.5
  63.5 11.9 %all-gather.5.cloned.1.call-done = bf16[1,768,1536]{2,1,0:T(8,128)(2,1)} async-done(((bf16[1,768,384]{2,1,0:T(8,128)(2,1)}), bf16[1,768,1536]{2,1,0:T(8,128)(2,1)}) %all-gather.5.cloned.1.call-update) | async-done | bytes 2359312 | tf_op jit(solution)/shard_map/all_gather | solution.py:57
  75.4 3.0 %fusion.2 = f32[4,128,1536]{2,1,0:T(8,128)S(1)} fusion(bf16[4,128,768]{2,1,0:T(8,128)(2,1)S(1)} %bitcast.38, bf16[1,768,1536]{2,1,0:T(8,128)(2,1)} %all-gather.5.cloned.1.call-done), kind=kOutput, calls=%fused_computation.4 | convolution fusion | flops 1207959552 | bytes 6291456 | tf_op jit(solution)/shard_map/dot_general | solution.py:61
  78.5 1.7 %copy-done.2 = f32[4,128,1536]{2,1,0:T(8,128)} copy-done((f32[4,128,1536]{2,1,0:T(8,128)}, f32[4,128,1536]{2,1,0:T(8,128)S(1)}, u32[]{:S(2)}) %copy-start.2) | copy-done | bytes 3145752
  80.2 1.6 %collective-permute-start = (bf16[4,64,1536]{2,1,0:T(8,128)(2,1)S(1)}, bf16[4,64,1536]{2,1,0:T(8,128)(2,1)S(1)}, u32[]{:S(2)}, u32[]{:S(2)}) collective-permute-start(bf16[4,64,1536]{2,1,0:T(8,128)(2,1)S(1)} %dynamic-slice_convert_fusion), channel_id=1, source_target_pairs={{0,4},{4,0},{8,12},{12,8},{1,5},{5,1},{9,13},{13,9},{2,6},{6,2},{1... | collective-permute-start | bytes 2359304 | tf_op jit(solution)/shard_map/ppermute | solution.py:14
  81.8 18.2 %collective-permute-done = bf16[4,64,1536]{2,1,0:T(8,128)(2,1)S(1)} collective-permute-done((bf16[4,64,1536]{2,1,0:T(8,128)(2,1)S(1)}, bf16[4,64,1536]{2,1,0:T(8,128)(2,1)S(1)}, u32[]{:S(2)}, u32[]{:S(2)}) %collective-permute-start) | collective-permute-done | bytes 786464 | tf_op jit(solution)/shard_map/ppermute | solution.py:14
  100.0 2.5 %add_convert_fusion = bf16[4,64,1536]{2,1,0:T(8,128)(2,1)} fusion(bf16[4,64,1536]{2,1,0:T(8,128)(2,1)S(1)} %collective-permute-done, f32[4,128,1536]{2,1,0:T(8,128)} %copy-done.2, s32[]{:T(128)S(6)} %select_n.26), kind=kLoop, calls=%fused_computation.10 | loop fusion | flops 1179648 | bytes 3145732 | tf_op jit(solution)/shard_map/convert_element_type | solution.py:66
  102.5 4.7 %all-to-all-start.1 = ((bf16[4,64,1536]{2,1,0:T(8,128)(2,1)}), bf16[4,64,1536]{2,1,0:T(8,128)(2,1)S(1)}, u32[]{:S(2)}, u32[]{:S(2)}) async-start(bf16[4,64,1536]{2,1,0:T(8,128)(2,1)} %add_convert_fusion), calls=%async_computation.1 | async-start | bytes 1572864 | tf_op jit(solution)/shard_map/all_to_all | solution.py:67
  107.3 19.6 %all-to-all-done.1 = bf16[4,64,1536]{2,1,0:T(8,128)(2,1)S(1)} async-done(((bf16[4,64,1536]{2,1,0:T(8,128)(2,1)}), bf16[4,64,1536]{2,1,0:T(8,128)(2,1)S(1)}, u32[]{:S(2)}, u32[]{:S(2)}) %all-to-all-start.1) | async-done | bytes 786464 | tf_op jit(solution)/shard_map/all_to_all | solution.py:67
  126.9 1.3 gather_fusion
  128.2 1.0 reshape.86
  129.2 2.2 %multiply_reduce_fusion = f32[128,1536]{1,0:T(8,128)S(1)} fusion(f32[128,2,1536]{2,1,0:T(2,128)S(1)} %reshape.86, f32[128,2]{1,0:T(8,128)S(1)} %copy.10), kind=kLoop, calls=%fused_computation.9 | loop fusion | flops 589824 | bytes 2360320 | tf_op jit(solution)/shard_map/reduce_sum | solution.py:70
  131.4 1.0 fusion.6
  132.4 0.5 rsqrt_multiply_fusion
  (24 shorter events, 0.5 us)
Async XLA Ops:
  7.2 1.5 %copy-start.4 = (s32[128,2]{0,1:T(2,128)S(1)}, s32[128,2]{0,1:T(2,128)}, u32[]{:S(2)}) copy-start(s32[128,2]{0,1:T(2,128)} %param.10) | copy-start | bytes 3076
  7.2 3.3 %copy-start = (bf16[128,1536]{1,0:T(8,128)(2,1)S(1)}, bf16[128,1536]{1,0:T(8,128)(2,1)}, u32[]{:S(2)}) copy-start(bf16[128,1536]{1,0:T(8,128)(2,1)} %param.7) | copy-start | bytes 1179652
  7.2 3.3 %copy-start.1 = (bf16[128,1536]{1,0:T(8,128)(2,1)S(1)}, bf16[128,1536]{1,0:T(8,128)(2,1)}, u32[]{:S(2)}) copy-start(bf16[128,1536]{1,0:T(8,128)(2,1)} %param.8) | copy-start | bytes 1179652
  7.2 3.5 %copy-start.3 = (f32[1536]{0:T(1024)S(1)}, f32[1536]{0:T(1024)}, u32[]{:S(2)}) copy-start(f32[1536]{0:T(1024)} %param.9) | copy-start | bytes 18436
  7.2 51.0 %all-gather.3.cloned.1.call-start = ((), (), s32[]{:S(2)}) async-start(), calls=%async_computation.2 | async-start | bytes 5898240 | tf_op jit(solution)/shard_map/all_gather | solution.py:56
  7.9 67.5 %all-gather.5.cloned.1.call-start = ((), (), s32[]{:S(2)}) async-start(), calls=%async_computation.3 | async-start | bytes 2949120 | tf_op jit(solution)/shard_map/all_gather | solution.py:57
  15.0 43.3 %all-to-all-start = ((bf16[4,128,1536]{2,1,0:T(8,128)(2,1)}), bf16[4,128,1536]{2,1,0:T(8,128)(2,1)S(1)}, u32[]{:S(2)}, u32[]{:S(2)}) async-start(bf16[4,128,1536]{2,1,0:T(8,128)(2,1)} %bitcast.4), calls=%async_computation | async-start | bytes 3145728 | tf_op jit(solution)/shard_map/all_to_all | solution.py:53
  78.5 1.7 %copy-start.2 = (f32[4,128,1536]{2,1,0:T(8,128)}, f32[4,128,1536]{2,1,0:T(8,128)S(1)}, u32[]{:S(2)}) copy-start(f32[4,128,1536]{2,1,0:T(8,128)S(1)} %fusion.2) | copy-start | bytes 9437188
  80.2 19.7 %collective-permute-start = (bf16[4,64,1536]{2,1,0:T(8,128)(2,1)S(1)}, bf16[4,64,1536]{2,1,0:T(8,128)(2,1)S(1)}, u32[]{:S(2)}, u32[]{:S(2)}) collective-permute-start(bf16[4,64,1536]{2,1,0:T(8,128)(2,1)S(1)} %dynamic-slice_convert_fusion), channel_id=1, source_target_pairs={{0,4},{4,0},{8,12},{12,8},{1,5},{5,1},{9,13},{13,9},{2,6},{6,2},{1... | collective-permute-start | bytes 2359304 | tf_op jit(solution)/shard_map/ppermute | solution.py:14
  102.5 4.7 %copy-start.5 = (f32[128,2]{0,1:T(2,128)S(1)}, f32[128,2]{0,1:T(2,128)}, u32[]{:S(2)}) copy-start(f32[128,2]{0,1:T(2,128)} %param.11) | copy-start | bytes 3076
  102.5 24.4 %all-to-all-start.1 = ((bf16[4,64,1536]{2,1,0:T(8,128)(2,1)}), bf16[4,64,1536]{2,1,0:T(8,128)(2,1)S(1)}, u32[]{:S(2)}, u32[]{:S(2)}) async-start(bf16[4,64,1536]{2,1,0:T(8,128)(2,1)} %add_convert_fusion), calls=%async_computation.1 | async-start | bytes 1572864 | tf_op jit(solution)/shard_map/all_to_all | solution.py:67
Sparse Core Ops, SparseCore 0:
  9.6 40.1 all-gather.2
  51.4 24.0 all-gather.4
where the time goes:
time: 140 us
  waiting for transfers between devices  88 us (63%)
  between operations  14.2 us (10%)
  starting transfers between devices  12.7 us (9%)
  local copies, waits for them, and re-layouts  8.98 us (6%)
  other arithmetic  8.03 us (6%)
  matrix products  7.83 us (6%)
    all_to_all x1, waiting for transfers between devices, shards(): lax.all_to_all(doubled, 'ep', split_axis=0, concat_axis=0, tiled=True)  37 us
    all_to_all x1, waiting for transfers between devices, shards(): lax.all_to_all(summed, 'ep', split_axis=0, concat_axis=0, tiled=True)  19.6 us
    ppermute x1, waiting for transfers between devices, swapped(): return lax.ppermute(value, axis, pairs)  18.2 us
    all_gather x1, waiting for transfers between devices, shards(): lax.all_gather(w_down, 'fsdp', axis=2, tiled=True)  11.9 us
    all_to_all x1, starting transfers between devices, shards(): lax.all_to_all(doubled, 'ep', split_axis=0, concat_axis=0, tiled=True)  6.32 us
    dot_general x1, matrix products, shards(): jnp.dot(slot_rows, full_up[0], preferred_element_type=jnp.float32)  4.79 us
    all_to_all x1, starting transfers between devices, shards(): lax.all_to_all(summed, 'ep', split_axis=0, concat_axis=0, tiled=True)  4.73 us
    dot_general x1, matrix products, shards(): jnp.dot(activated, full_down[0], preferred_element_type=jnp.float32)  3.05 us
  transfers between devices with their start and end apart: 5, of which 4 were waited for; matrix products, arithmetic and copies ran while one was open for 8% of the time, Pallas kernels for 0%

commit v1 on v0

--- a/solution.py
+++ b/solution.py
@@ -1,6 +1,10 @@
+import functools
+
 import jax
 import jax.numpy as jnp
 from jax import lax
+from jax.experimental import pallas as pl
+from jax.experimental.pallas import tpu as pltpu
 from jax.sharding import PartitionSpec as P
 
 norm_eps = 1e-05
@@ -22,7 +26,7 @@
     )
 
 
-def shards(layer_in, attn_out, norm_gain, expert_ids, gate_weights, w_gate_up, w_down):
+def routed_shards(layer_in, attn_out, norm_gain, expert_ids, gate_weights, w_gate_up, w_down):
     tokens, features = layer_in.shape
     routes = expert_ids.shape[1]
     devices_ep = lax.axis_size("ep")
@@ -78,6 +82,157 @@
     return (updated.astype(jnp.bfloat16), similarity)
 
 
+def kernel_call(body, outs, scratch=(), flops=0, moved=0):
+    return pl.pallas_call(
+        body,
+        out_shape=outs,
+        scratch_shapes=list(scratch),
+        compiler_params=pltpu.CompilerParams(vmem_limit_bytes=40 * 2**20),
+        cost_estimate=pl.CostEstimate(flops=flops, bytes_accessed=moved, transcendentals=0),
+    )
+
+
+def dot(left, right):
+    return jnp.dot(left, right, preferred_element_type=jnp.float32)
+
+
+def project_body(count, *refs):
+    tokens_in = refs[:count]
+    own, core_own, near, far, core_near, core_far, hidden_out, rows = refs[count:]
+    tokens, half_depth = tokens_in[0].shape[0], near.shape[0]
+    width = own.shape[1]
+    for block in range(count):
+        rows[block * tokens : (block + 1) * tokens, :] = tokens_in[block][...]
+    spot = lax.axis_index("fsdp")
+    on_gate = spot < 2
+    group = lax.axis_index("groups")
+    near_depth = pl.ds(pl.multiple_of(group * half_depth, half_depth), half_depth)
+    far_depth = pl.ds(pl.multiple_of((1 - group) * half_depth, half_depth), half_depth)
+    for mine, first, second, hidden_block in (
+        (own, near, far, spot % 2),
+        (core_own, core_near, core_far, 1 - spot % 2),
+    ):
+        here = dot(rows[...], mine[...])
+        there = dot(rows[:, near_depth], first[...]) + dot(rows[:, far_depth], second[...])
+        gate_part = jnp.where(on_gate, here, there)
+        up_part = jnp.where(on_gate, there, here)
+        columns = pl.ds(pl.multiple_of(hidden_block * width, width), width)
+        hidden_out[:, columns] = (
+            gate_part * jax.nn.sigmoid(glu_alpha * gate_part) * (up_part + 1.0)
+        ).astype(jnp.bfloat16)
+
+
+def project(blocks, panels):
+    tokens, features = blocks[0].shape
+    rows = len(blocks) * tokens
+    hidden = 2 * panels[0].shape[1]
+    return kernel_call(
+        functools.partial(project_body, len(blocks)),
+        jax.ShapeDtypeStruct((rows, hidden), jnp.bfloat16),
+        [pltpu.VMEM((rows, features), jnp.bfloat16)],
+        4 * rows * features * hidden,
+        4 * features * hidden + 2 * rows * (features + hidden),
+    )(*blocks, *panels)
+
+
+def lower_body(count, hidden, *refs):
+    panels, outs = refs[:4], refs[4:]
+    tokens, width = outs[0].shape[0], panels[0].shape[1]
+    spot = lax.axis_index("fsdp")
+    for panel, source in zip(panels, (spot, spot ^ 1, spot ^ 2, spot ^ 3)):
+        part = dot(hidden[...], panel[...])
+        columns = pl.ds(pl.multiple_of(source * width, width), width)
+        for block in range(count):
+            outs[block][:, columns] = part[block * tokens : (block + 1) * tokens].astype(
+                outs[block].dtype
+            )
+
+
+def lower(hidden, panels, kinds):
+    count = len(kinds)
+    tokens = hidden.shape[0] // count
+    features = 4 * panels[0].shape[1]
+    return kernel_call(
+        functools.partial(lower_body, count),
+        tuple(jax.ShapeDtypeStruct((tokens, features), kind) for kind in kinds),
+        (),
+        2 * hidden.shape[0] * hidden.shape[1] * features,
+        2 * hidden.shape[1] * features + 4 * hidden.shape[0] * features,
+    )(hidden, *panels)
+
+
+def finish_body(layer_in, attn_out, ids, weights, kept, partner, other, layer_out, similarity):
+    inputs = layer_in[...].astype(jnp.float32)
+    residual = inputs + attn_out[...].astype(jnp.float32)
+    mine = (kept[...] + partner[...].astype(jnp.float32)).astype(jnp.bfloat16).astype(jnp.float32)
+    own_expert = lax.axis_index("ep") // 2
+    named = ids[...] == own_expert
+    own_gate = jnp.sum(jnp.where(named, weights[...], 0.0), axis=1, keepdims=True)
+    other_gate = jnp.sum(jnp.where(named, 0.0, weights[...]), axis=1, keepdims=True)
+    updated = residual + (own_gate * mine + other_gate * other[...].astype(jnp.float32))
+    layer_out[...] = updated.astype(jnp.bfloat16)
+    value = (
+        jnp.sum(inputs * updated, axis=-1, keepdims=True)
+        * lax.rsqrt(jnp.sum(inputs * inputs, axis=-1, keepdims=True) + cos_eps)
+        * lax.rsqrt(jnp.sum(updated * updated, axis=-1, keepdims=True) + cos_eps)
+    )
+    tokens = value.shape[0]
+    similarity[...] = jnp.broadcast_to(value, (tokens, tokens)).T[0:1, :]
+
+
+def dense_shards(layer_in, attn_out, norm_gain, expert_ids, gate_weights, w_gate_up, w_down):
+    tokens, features = layer_in.shape
+    own_up, own_down = w_gate_up[0], w_down[0]
+    half_depth = features // 2
+    group = lax.axis_index("groups")
+    first_half = lax.dynamic_slice_in_dim(own_up, group * half_depth, half_depth, 0)
+    near = swapped(first_half, "fsdp", 1)
+    x_down = swapped(own_down, "fsdp", 1)
+    far = swapped(near, "groups", 0)
+    core_up, core_down = swapped(own_up, "fsdp", 0), swapped(own_down, "fsdp", 0)
+    core_near, core_far = swapped(near, "fsdp", 0), swapped(far, "fsdp", 0)
+    core_x_down = swapped(x_down, "fsdp", 0)
+    up_panels = (own_up, core_up, near, far, core_near, core_far)
+    down_panels = (own_down, core_down, x_down, core_x_down)
+
+    inputs = layer_in.astype(jnp.float32)
+    residual = inputs + attn_out.astype(jnp.float32)
+    mean_square = jnp.mean(residual * residual, axis=-1, keepdims=True)
+    normed = (residual * lax.rsqrt(mean_square + norm_eps) * norm_gain[None, :]).astype(
+        jnp.bfloat16
+    )
+    two = swapped(normed, "ep", 1)
+    one = swapped(normed, "ep", 0)
+    three = swapped(two, "ep", 0)
+    early = project((normed, one, two), up_panels)
+    kept, sent_one, kept_two = lower(
+        early, down_panels, (jnp.float32, jnp.bfloat16, jnp.float32)
+    )
+    (sent_three,) = lower(project((three,), up_panels), down_panels, (jnp.bfloat16,))
+    got_two = swapped(sent_three, "ep", 0)
+    joined = (kept_two + got_two.astype(jnp.float32)).astype(jnp.bfloat16)
+    other = swapped(joined, "ep", 1)
+    partner = swapped(sent_one, "ep", 0)
+    layer_out, similarity = kernel_call(
+        finish_body,
+        (
+            jax.ShapeDtypeStruct((tokens, features), jnp.bfloat16),
+            jax.ShapeDtypeStruct((1, tokens), jnp.float32),
+        ),
+        (),
+        20 * tokens * features,
+        16 * tokens * features,
+    )(layer_in, attn_out, expert_ids, gate_weights, kept, partner, other)
+    return layer_out, similarity.reshape(tokens)
+
+
+def shards(*args):
+    sizes = tuple(lax.axis_size(axis) for axis in ("groups", "ep", "fsdp"))
+    routes = args[3].shape[1]
+    every_expert = sizes[1] == 2 * routes
+    return (dense_shards if every_expert and sizes == (2, 4, 4) else routed_shards)(*args)
+
+
 def solution(mesh):
     placed = (
         P(("groups", "ep", "fsdp"), None),

time: 140 us -> 77.5 us (0.55)
  waiting for transfers between devices: 88 us -> 50.3 us
  between operations: 14.2 us -> 0.77 us
  matrix products: 7.83 us -> 0 us
  other arithmetic: 8.03 us -> 0.45 us
  local copies, waits for them, and re-layouts: 8.98 us -> 1.46 us
  Pallas kernels: 0 us -> 6.86 us
  starting transfers between devices: 12.7 us -> 17.6 us
    all_to_all x2 -> x0, waiting for transfers between devices: 56.5 us -> none  [the longest x1 37 us: shards(): lax.all_to_all(doubled, 'ep', split_axis=0, concat_axis=0, tiled=True)]
    ppermute x1 -> x14, waiting for transfers between devices: 18.2 us -> 50.3 us  [swapped(): return lax.ppermute(value, axis, pairs)]
    ppermute x1 -> x14, starting transfers between devices: 1.55 us -> 17.6 us  [swapped(): return lax.ppermute(value, axis, pairs)]
    all_gather x2 -> x0, waiting for transfers between devices: 11.9 us -> none  [the longest x1 11.9 us: shards(): lax.all_gather(w_down, 'fsdp', axis=2, tiled=True)]
    all_to_all x2 -> x0, starting transfers between devices: 11 us -> none  [the longest x1 6.32 us: shards(): lax.all_to_all(doubled, 'ep', split_axis=0, concat_axis=0, tiled=True)]
    dot_general x2 -> x0, matrix products: 7.83 us -> none  [the longest x1 4.79 us: shards(): jnp.dot(slot_rows, full_up[0], preferred_element_type=jnp.float32)]
    pallas_call x0 -> x5, Pallas kernels: none -> 6.86 us  [the longest x2 3.7 us: project(): kernel_call(functools.partial(project_body, len(blocks)), jax.ShapeDtypeS...]
    reduce_sum x4 -> x1, other arithmetic: 3.47 us -> 0.21 us  [dense_shards(): mean_square = jnp.mean(residual * residual, axis=-1, keepdims=True)]
  transfers between devices with their start and end apart: 5 -> 14, of which waited for: 4 -> 9; matrix products, arithmetic and copies ran while one was open for 8% -> 1% of each run, Pallas kernels for 0% -> 7%
where the time goes in v1:
time: 77.5 us; the launch traced here: 77.4 us
  waiting for transfers between devices  50.3 us (65%)
  starting transfers between devices  17.6 us (23%)
  Pallas kernels  6.86 us (9%)
  local copies, waits for them, and re-layouts  1.46 us (2%)
    ppermute x14, waiting for transfers between devices, swapped(): return lax.ppermute(value, axis, pairs)  50.3 us
    ppermute x14, starting transfers between devices, swapped(): return lax.ppermute(value, axis, pairs)  17.6 us
    pallas_call x2, Pallas kernels, project(): kernel_call(functools.partial(project_body, len(blocks)), jax.ShapeDtypeS...  3.7 us
    pallas_call x2, Pallas kernels, lower(): kernel_call(functools.partial(lower_body, count), tuple((jax.ShapeDtypeSt...  1.95 us
  transfers between devices with their start and end apart: 14, of which 9 were waited for; matrix products, arithmetic and copies ran while one was open for 1% of the time, Pallas kernels for 7%

profile of v1, /device:TPU:0, one launch (start us, length us, event | category | flops | bytes accessed | tf_op | source)
XLA Modules:
  0.0 77.4 jit_solution(16412711443709073719)
XLA Ops:
  0.7 1.2 %dynamic-slice_bitcast_fusion = bf16[768,384]{1,0:T(8,128)(2,1)S(1)} fusion(bf16[1,1536,384]{2,1,0:T(8,128)(2,1)} %param.12, s32[]{:T(128)S(6)} %select_n.3), kind=kLoop, calls=%fused_computation.4 | loop fusion | bytes 1179652 | tf_op jit(solution)/shard_map/dynamic_slice | solution.py:188
  1.9 0.0 copy-start.2
  1.9 0.0 copy-start.3
  1.9 3.0 %collective-permute-start.3 = (bf16[768,384]{1,0:T(8,128)(2,1)S(1)}, bf16[768,384]{1,0:T(8,128)(2,1)S(1)}, u32[]{:S(2)}, u32[]{:S(2)}) collective-permute-start(bf16[768,384]{1,0:T(8,128)(2,1)S(1)} %dynamic-slice_bitcast_fusion), channel_id=1, source_target_pairs={{0,2},{1,3},{2,0},{3,1},{4,6},{5,7},{6,4},{7,5},{8,10},{9,11},{10,... | collective-permute-start | bytes 1769480 | tf_op jit(solution)/shard_map/ppermute | solution.py:18
  4.9 0.2 multiply_reduce_fusion
  5.1 0.2 multiply_convert_fusion.refs_0_
  5.3 2.7 %collective-permute-start.1 = (bf16[128,1536]{1,0:T(8,128)(2,1)S(1)}, bf16[128,1536]{1,0:T(8,128)(2,1)S(1)}, u32[]{:S(2)}, u32[]{:S(2)}) collective-permute-start(bf16[128,1536]{1,0:T(8,128)(2,1)S(1)} %multiply_convert_fusion.refs_0_), channel_id=1, source_target_pairs={{0,8},{4,12},{8,0},{12,4},{1,9},{5,13},{9,1},{13,5},{2,10},{6,14},... | collective-permute-start | bytes 1179656 | tf_op jit(solution)/shard_map/ppermute | solution.py:18
  8.0 10.3 %collective-permute-done.3.refs_5_.refs_3_ = bf16[768,384]{1,0:T(8,128)(2,1)S(1)} collective-permute-done((bf16[768,384]{1,0:T(8,128)(2,1)S(1)}, bf16[768,384]{1,0:T(8,128)(2,1)S(1)}, u32[]{:S(2)}, u32[]{:S(2)}) %collective-permute-start.3) | collective-permute-done | bytes 589856 | tf_op jit(solution)/shard_map/ppermute | solution.py:18
  18.2 1.8 %collective-permute-start.4 = (bf16[768,384]{1,0:T(8,128)(2,1)S(1)}, bf16[768,384]{1,0:T(8,128)(2,1)S(1)}, u32[]{:S(2)}, u32[]{:S(2)}) collective-permute-start(bf16[768,384]{1,0:T(8,128)(2,1)S(1)} %collective-permute-done.3.refs_5_.refs_3_), channel_id=1, source_target_pairs={{0,16},{16,0},{1,17},{17,1},{2,18},{18,2},{3,19},{19,3},{4,20},{20... | collective-permute-start | bytes 1769480 | tf_op jit(solution)/shard_map/ppermute | solution.py:18
  20.0 1.5 %collective-permute-start.8 = (bf16[768,384]{1,0:T(8,128)(2,1)S(1)}, bf16[768,384]{1,0:T(8,128)(2,1)S(1)}, u32[]{:S(2)}, u32[]{:S(2)}) collective-permute-start(bf16[768,384]{1,0:T(8,128)(2,1)S(1)} %bitcast.8), channel_id=1, source_target_pairs={{0,2},{1,3},{2,0},{3,1},{4,6},{5,7},{6,4},{7,5},{8,10},{9,11},{10,... | collective-permute-start | bytes 1769480 | tf_op jit(solution)/shard_map/ppermute | solution.py:18
  21.5 3.8 %collective-permute-done.1.refs_2_ = bf16[128,1536]{1,0:T(8,128)(2,1)S(1)} collective-permute-done((bf16[128,1536]{1,0:T(8,128)(2,1)S(1)}, bf16[128,1536]{1,0:T(8,128)(2,1)S(1)}, u32[]{:S(2)}, u32[]{:S(2)}) %collective-permute-start.1) | collective-permute-done | bytes 393248 | tf_op jit(solution)/shard_map/ppermute | solution.py:18
  25.3 0.7 collective-permute-start.11
  25.9 6.8 %collective-permute-done.4.refs_6_.refs_4_ = bf16[768,384]{1,0:T(8,128)(2,1)S(1)} collective-permute-done((bf16[768,384]{1,0:T(8,128)(2,1)S(1)}, bf16[768,384]{1,0:T(8,128)(2,1)S(1)}, u32[]{:S(2)}, u32[]{:S(2)}) %collective-permute-start.4) | collective-permute-done | bytes 589856 | tf_op jit(solution)/shard_map/ppermute | solution.py:18
  32.7 1.2 %collective-permute-done.8.refs_2_ = bf16[768,384]{1,0:T(8,128)(2,1)S(1)} collective-permute-done((bf16[768,384]{1,0:T(8,128)(2,1)S(1)}, bf16[768,384]{1,0:T(8,128)(2,1)S(1)}, u32[]{:S(2)}, u32[]{:S(2)}) %collective-permute-start.8) | collective-permute-done | bytes 589856 | tf_op jit(solution)/shard_map/ppermute | solution.py:18
  33.9 1.3 %collective-permute-done.11.refs_0_ = bf16[128,1536]{1,0:T(8,128)(2,1)S(1)} collective-permute-done((bf16[128,1536]{1,0:T(8,128)(2,1)S(1)}, bf16[128,1536]{1,0:T(8,128)(2,1)S(1)}, u32[]{:S(2)}, u32[]{:S(2)}) %collective-permute-start.11) | collective-permute-done | bytes 393248 | tf_op jit(solution)/shard_map/ppermute | solution.py:18
  35.2 1.7 %collective-permute-start = (bf16[128,1536]{1,0:T(8,128)(2,1)S(1)}, bf16[128,1536]{1,0:T(8,128)(2,1)S(1)}, u32[]{:S(2)}, u32[]{:S(2)}) collective-permute-start(bf16[128,1536]{1,0:T(8,128)(2,1)S(1)} %multiply_convert_fusion.refs_0_), channel_id=1, source_target_pairs={{0,4},{4,0},{8,12},{12,8},{1,5},{5,1},{9,13},{13,9},{2,6},{6,2},{1... | collective-permute-start | bytes 1179656 | tf_op jit(solution)/shard_map/ppermute | solution.py:18
  37.0 1.0 %shard_map.88.hidden = bf16[128,768]{1,0:T(8,128)(2,1)S(1)} custom-call(bf16[128,1536]{1,0:T(8,128)(2,1)S(1)} %collective-permute-done.11.refs_0_, bf16[1536,384]{1,0:T(8,128)(2,1)S(1)} %bitcast.6, bf16[1536,384]{1,0:T(8,128)(2,1)S(1)} %collective-permute-done.2.refs_4_.refs_2_, bf16[768,384]{1,0:T(8,128)(2,1)S(1)} %collective-permute-done.3.refs_5_.refs_3_, ...), custom_call_target="tpu_custom_call" | custom-call | flops 603979776 | bytes 5308416 | tf_op jit(solution)/shard_map/pallas_call | solution.py:129
  38.0 0.6 shard_map.89
  38.6 1.0 %collective-permute-start.12 = (bf16[128,1536]{1,0:T(8,128)(2,1)S(1)}, bf16[128,1536]{1,0:T(8,128)(2,1)S(1)}, u32[]{:S(2)}, u32[]{:S(2)}) collective-permute-start(bf16[128,1536]{1,0:T(8,128)(2,1)S(1)} %shard_map.89), channel_id=1, source_target_pairs={{0,4},{4,0},{8,12},{12,8},{1,5},{5,1},{9,13},{13,9},{2,6},{6,2},{1... | collective-permute-start | bytes 1179656 | tf_op jit(solution)/shard_map/ppermute | solution.py:18
  39.6 7.5 %collective-permute-done.refs_1_ = bf16[128,1536]{1,0:T(8,128)(2,1)S(1)} collective-permute-done((bf16[128,1536]{1,0:T(8,128)(2,1)S(1)}, bf16[128,1536]{1,0:T(8,128)(2,1)S(1)}, u32[]{:S(2)}, u32[]{:S(2)}) %collective-permute-start) | collective-permute-done | bytes 393248 | tf_op jit(solution)/shard_map/ppermute | solution.py:18
  47.1 2.7 %shard_map.86.hidden = bf16[384,768]{1,0:T(8,128)(2,1)S(1)} custom-call(bf16[128,1536]{1,0:T(8,128)(2,1)S(1)} %multiply_convert_fusion.refs_0_, bf16[128,1536]{1,0:T(8,128)(2,1)S(1)} %collective-permute-done.refs_1_, bf16[128,1536]{1,0:T(8,128)(2,1)S(1)} %collective-permute-done.1.refs_2_, bf16[1536,384]{1,0:T(8,128)(2,1)S(1)} %bitcast.7, ...), custom_call_target="tpu_custom_call" | custom-call | flops 1811939328 | bytes 6488064 | tf_op jit(solution)/shard_map/pallas_call | solution.py:129
  49.8 1.4 %shard_map.87 = (f32[128,1536]{1,0:T(8,128)S(1)}, bf16[128,1536]{1,0:T(8,128)(2,1)S(1)}, f32[128,1536]{1,0:T(8,128)S(1)}) custom-call(bf16[384,768]{1,0:T(8,128)(2,1)S(1)} %shard_map.86.hidden, bf16[768,384]{1,0:T(8,128)(2,1)S(1)} %bitcast.11, bf16[768,384]{1,0:T(8,128)(2,1)S(1)} %collective-permute-done.7.refs_1_, ...), custom_call_target="tpu_custom_call" | custom-call | flops 905969664 | bytes 4718592 | tf_op jit(solution)/shard_map/pallas_call | solution.py:155
  51.2 0.0 copy-start.5
  51.2 1.8 %collective-permute-start.10 = (bf16[128,1536]{1,0:T(8,128)(2,1)S(1)}, bf16[128,1536]{1,0:T(8,128)(2,1)S(1)}, u32[]{:S(2)}, u32[]{:S(2)}) collective-permute-start(bf16[128,1536]{1,0:T(8,128)(2,1)S(1)} %get-tuple-element.8), channel_id=1, source_target_pairs={{0,4},{4,0},{8,12},{12,8},{1,5},{5,1},{9,13},{13,9},{2,6},{6,2},{1... | collective-permute-start | bytes 1179656 | tf_op jit(solution)/shard_map/ppermute | solution.py:18
  53.1 2.5 %collective-permute-done.12 = bf16[128,1536]{1,0:T(8,128)(2,1)S(1)} collective-permute-done((bf16[128,1536]{1,0:T(8,128)(2,1)S(1)}, bf16[128,1536]{1,0:T(8,128)(2,1)S(1)}, u32[]{:S(2)}, u32[]{:S(2)}) %collective-permute-start.12) | collective-permute-done | bytes 393248 | tf_op jit(solution)/shard_map/ppermute | solution.py:18
  55.6 0.1 add_convert_fusion
  55.6 3.4 %collective-permute-start.13 = (bf16[128,1536]{1,0:T(8,128)(2,1)S(1)}, bf16[128,1536]{1,0:T(8,128)(2,1)S(1)}, u32[]{:S(2)}, u32[]{:S(2)}) collective-permute-start(bf16[128,1536]{1,0:T(8,128)(2,1)S(1)} %add_convert_fusion), channel_id=1, source_target_pairs={{0,8},{4,12},{8,0},{12,4},{1,9},{5,13},{9,1},{13,5},{2,10},{6,14},... | collective-permute-start | bytes 1179656 | tf_op jit(solution)/shard_map/ppermute | solution.py:18
  59.1 0.1 copy.9.ids
  59.2 0.1 copy.10.weights
  59.3 11.5 %collective-permute-done.10.partner = bf16[128,1536]{1,0:T(8,128)(2,1)S(1)} collective-permute-done((bf16[128,1536]{1,0:T(8,128)(2,1)S(1)}, bf16[128,1536]{1,0:T(8,128)(2,1)S(1)}, u32[]{:S(2)}, u32[]{:S(2)}) %collective-permute-start.10) | collective-permute-done | bytes 393248 | tf_op jit(solution)/shard_map/ppermute | solution.py:18
  70.8 5.4 %collective-permute-done.13.other = bf16[128,1536]{1,0:T(8,128)(2,1)S(1)} collective-permute-done((bf16[128,1536]{1,0:T(8,128)(2,1)S(1)}, bf16[128,1536]{1,0:T(8,128)(2,1)S(1)}, u32[]{:S(2)}, u32[]{:S(2)}) %collective-permute-start.13) | collective-permute-done | bytes 393248 | tf_op jit(solution)/shard_map/ppermute | solution.py:18
  76.2 1.2 %shard_map.90 = (bf16[128,1536]{1,0:T(8,128)(2,1)}, f32[1,128]{1,0:T(1,128)}) custom-call(bf16[128,1536]{1,0:T(8,128)(2,1)S(1)} %copy-done, bf16[128,1536]{1,0:T(8,128)(2,1)S(1)} %copy-done.1, s32[128,2]{1,0:T(8,128)S(1)} %copy.9.ids, f32[128,2]{1,0:T(8,128)S(1)} %copy.10.weights, f32[128,1536]{1,0:T(8,128)S(1)} %get-tuple-element.7.kept, ...), custom_call_target="tpu_custom_call" | custom-call | flops 3932160 | bytes 3145728 | tf_op jit(solution)/shard_map/pallas_call | solution.py:216
  (22 shorter events, 0.1 us)
Async XLA Ops:
  0.6 4.3 %copy-start.1 = (bf16[128,1536]{1,0:T(8,128)(2,1)S(1)}, bf16[128,1536]{1,0:T(8,128)(2,1)}, u32[]{:S(2)}) copy-start(bf16[128,1536]{1,0:T(8,128)(2,1)} %attn_out.1) | copy-start | bytes 1179652
  0.6 4.3 %copy-start = (bf16[128,1536]{1,0:T(8,128)(2,1)S(1)}, bf16[128,1536]{1,0:T(8,128)(2,1)}, u32[]{:S(2)}) copy-start(bf16[128,1536]{1,0:T(8,128)(2,1)} %layer_in.1) | copy-start | bytes 1179652
  0.6 4.5 %copy-start.4 = (f32[1536]{0:T(1024)S(1)}, f32[1536]{0:T(1024)}, u32[]{:S(2)}) copy-start(f32[1536]{0:T(1024)} %param.9) | copy-start | bytes 18436
  1.9 6.1 %copy-start.2 = (bf16[1,1536,384]{2,1,0:T(8,128)(2,1)S(1)}, bf16[1,1536,384]{2,1,0:T(8,128)(2,1)}, u32[]{:S(2)}) copy-start(bf16[1,1536,384]{2,1,0:T(8,128)(2,1)} %param.12) | copy-start | bytes 3538948
  1.9 18.1 %copy-start.3 = (bf16[1,768,384]{2,1,0:T(8,128)(2,1)S(1)}, bf16[1,768,384]{2,1,0:T(8,128)(2,1)}, u32[]{:S(2)}) copy-start(bf16[1,768,384]{2,1,0:T(8,128)(2,1)} %param.13) | copy-start | bytes 1769476
  1.9 16.3 %collective-permute-start.3 = (bf16[768,384]{1,0:T(8,128)(2,1)S(1)}, bf16[768,384]{1,0:T(8,128)(2,1)S(1)}, u32[]{:S(2)}, u32[]{:S(2)}) collective-permute-start(bf16[768,384]{1,0:T(8,128)(2,1)S(1)} %dynamic-slice_bitcast_fusion), channel_id=1, source_target_pairs={{0,2},{1,3},{2,0},{3,1},{4,6},{5,7},{6,4},{7,5},{8,10},{9,11},{10,... | collective-permute-start | bytes 1769480 | tf_op jit(solution)/shard_map/ppermute | solution.py:18
  5.3 20.0 %collective-permute-start.1 = (bf16[128,1536]{1,0:T(8,128)(2,1)S(1)}, bf16[128,1536]{1,0:T(8,128)(2,1)S(1)}, u32[]{:S(2)}, u32[]{:S(2)}) collective-permute-start(bf16[128,1536]{1,0:T(8,128)(2,1)S(1)} %multiply_convert_fusion.refs_0_), channel_id=1, source_target_pairs={{0,8},{4,12},{8,0},{12,4},{1,9},{5,13},{9,1},{13,5},{2,10},{6,14},... | collective-permute-start | bytes 1179656 | tf_op jit(solution)/shard_map/ppermute | solution.py:18
  7.9 29.0 %collective-permute-start.2 = (bf16[1536,384]{1,0:T(8,128)(2,1)S(1)}, bf16[1536,384]{1,0:T(8,128)(2,1)S(1)}, u32[]{:S(2)}, u32[]{:S(2)}) collective-permute-start(bf16[1536,384]{1,0:T(8,128)(2,1)S(1)} %bitcast.5), channel_id=1, source_target_pairs={{0,1},{1,0},{2,3},{3,2},{4,5},{5,4},{6,7},{7,6},{8,9},{9,8},{10,11... | collective-permute-start | bytes 3538952 | tf_op jit(solution)/shard_map/ppermute | solution.py:18
  18.2 14.5 %collective-permute-start.4 = (bf16[768,384]{1,0:T(8,128)(2,1)S(1)}, bf16[768,384]{1,0:T(8,128)(2,1)S(1)}, u32[]{:S(2)}, u32[]{:S(2)}) collective-permute-start(bf16[768,384]{1,0:T(8,128)(2,1)S(1)} %collective-permute-done.3.refs_5_.refs_3_), channel_id=1, source_target_pairs={{0,16},{16,0},{1,17},{17,1},{2,18},{18,2},{3,19},{19,3},{4,20},{20... | collective-permute-start | bytes 1769480 | tf_op jit(solution)/shard_map/ppermute | solution.py:18
  20.0 13.9 %collective-permute-start.8 = (bf16[768,384]{1,0:T(8,128)(2,1)S(1)}, bf16[768,384]{1,0:T(8,128)(2,1)S(1)}, u32[]{:S(2)}, u32[]{:S(2)}) collective-permute-start(bf16[768,384]{1,0:T(8,128)(2,1)S(1)} %bitcast.8), channel_id=1, source_target_pairs={{0,2},{1,3},{2,0},{3,1},{4,6},{5,7},{6,4},{7,5},{8,10},{9,11},{10,... | collective-permute-start | bytes 1769480 | tf_op jit(solution)/shard_map/ppermute | solution.py:18
  25.3 10.0 %collective-permute-start.11 = (bf16[128,1536]{1,0:T(8,128)(2,1)S(1)}, bf16[128,1536]{1,0:T(8,128)(2,1)S(1)}, u32[]{:S(2)}, u32[]{:S(2)}) collective-permute-start(bf16[128,1536]{1,0:T(8,128)(2,1)S(1)} %collective-permute-done.1.refs_2_), channel_id=1, source_target_pairs={{0,4},{4,0},{8,12},{12,8},{1,5},{5,1},{9,13},{13,9},{2,6},{6,2},{1... | collective-permute-start | bytes 1179656 | tf_op jit(solution)/shard_map/ppermute | solution.py:18
  25.9 9.3 %collective-permute-start.5 = (bf16[768,384]{1,0:T(8,128)(2,1)S(1)}, bf16[768,384]{1,0:T(8,128)(2,1)S(1)}, u32[]{:S(2)}, u32[]{:S(2)}) collective-permute-start(bf16[768,384]{1,0:T(8,128)(2,1)S(1)} %collective-permute-done.3.refs_5_.refs_3_), channel_id=1, source_target_pairs={{0,1},{1,0},{2,3},{3,2},{4,5},{5,4},{6,7},{7,6},{8,9},{9,8},{10,11... | collective-permute-start | bytes 1769480 | tf_op jit(solution)/shard_map/ppermute | solution.py:18
  32.7 4.2 %collective-permute-start.6 = (bf16[768,384]{1,0:T(8,128)(2,1)S(1)}, bf16[768,384]{1,0:T(8,128)(2,1)S(1)}, u32[]{:S(2)}, u32[]{:S(2)}) collective-permute-start(bf16[768,384]{1,0:T(8,128)(2,1)S(1)} %collective-permute-done.4.refs_6_.refs_4_), channel_id=1, source_target_pairs={{0,1},{1,0},{2,3},{3,2},{4,5},{5,4},{6,7},{7,6},{8,9},{9,8},{10,11... | collective-permute-start | bytes 1769480 | tf_op jit(solution)/shard_map/ppermute | solution.py:18
  33.9 4.1 %collective-permute-start.7 = (bf16[768,384]{1,0:T(8,128)(2,1)S(1)}, bf16[768,384]{1,0:T(8,128)(2,1)S(1)}, u32[]{:S(2)}, u32[]{:S(2)}) collective-permute-start(bf16[768,384]{1,0:T(8,128)(2,1)S(1)} %bitcast.9), channel_id=1, source_target_pairs={{0,1},{1,0},{2,3},{3,2},{4,5},{5,4},{6,7},{7,6},{8,9},{9,8},{10,11... | collective-permute-start | bytes 1769480 | tf_op jit(solution)/shard_map/ppermute | solution.py:18
  35.2 2.8 %collective-permute-start.9 = (bf16[768,384]{1,0:T(8,128)(2,1)S(1)}, bf16[768,384]{1,0:T(8,128)(2,1)S(1)}, u32[]{:S(2)}, u32[]{:S(2)}) collective-permute-start(bf16[768,384]{1,0:T(8,128)(2,1)S(1)} %collective-permute-done.8.refs_2_), channel_id=1, source_target_pairs={{0,1},{1,0},{2,3},{3,2},{4,5},{5,4},{6,7},{7,6},{8,9},{9,8},{10,11... | collective-permute-start | bytes 1769480 | tf_op jit(solution)/shard_map/ppermute | solution.py:18
  35.2 11.9 %collective-permute-start = (bf16[128,1536]{1,0:T(8,128)(2,1)S(1)}, bf16[128,1536]{1,0:T(8,128)(2,1)S(1)}, u32[]{:S(2)}, u32[]{:S(2)}) collective-permute-start(bf16[128,1536]{1,0:T(8,128)(2,1)S(1)} %multiply_convert_fusion.refs_0_), channel_id=1, source_target_pairs={{0,4},{4,0},{8,12},{12,8},{1,5},{5,1},{9,13},{13,9},{2,6},{6,2},{1... | collective-permute-start | bytes 1179656 | tf_op jit(solution)/shard_map/ppermute | solution.py:18
  38.6 17.0 %collective-permute-start.12 = (bf16[128,1536]{1,0:T(8,128)(2,1)S(1)}, bf16[128,1536]{1,0:T(8,128)(2,1)S(1)}, u32[]{:S(2)}, u32[]{:S(2)}) collective-permute-start(bf16[128,1536]{1,0:T(8,128)(2,1)S(1)} %shard_map.89), channel_id=1, source_target_pairs={{0,4},{4,0},{8,12},{12,8},{1,5},{5,1},{9,13},{13,9},{2,6},{6,2},{1... | collective-permute-start | bytes 1179656 | tf_op jit(solution)/shard_map/ppermute | solution.py:18
  51.2 7.9 %copy-start.5 = (s32[128,2]{0,1:T(2,128)S(1)}, s32[128,2]{0,1:T(2,128)}, u32[]{:S(2)}) copy-start(s32[128,2]{0,1:T(2,128)} %param.10) | copy-start | bytes 3076
  51.2 8.0 %copy-start.6 = (f32[128,2]{0,1:T(2,128)S(1)}, f32[128,2]{0,1:T(2,128)}, u32[]{:S(2)}) copy-start(f32[128,2]{0,1:T(2,128)} %param.11) | copy-start | bytes 3076
  51.2 19.6 %collective-permute-start.10 = (bf16[128,1536]{1,0:T(8,128)(2,1)S(1)}, bf16[128,1536]{1,0:T(8,128)(2,1)S(1)}, u32[]{:S(2)}, u32[]{:S(2)}) collective-permute-start(bf16[128,1536]{1,0:T(8,128)(2,1)S(1)} %get-tuple-element.8), channel_id=1, source_target_pairs={{0,4},{4,0},{8,12},{12,8},{1,5},{5,1},{9,13},{13,9},{2,6},{6,2},{1... | collective-permute-start | bytes 1179656 | tf_op jit(solution)/shard_map/ppermute | solution.py:18
  55.6 20.5 %collective-permute-start.13 = (bf16[128,1536]{1,0:T(8,128)(2,1)S(1)}, bf16[128,1536]{1,0:T(8,128)(2,1)S(1)}, u32[]{:S(2)}, u32[]{:S(2)}) collective-permute-start(bf16[128,1536]{1,0:T(8,128)(2,1)S(1)} %add_convert_fusion), channel_id=1, source_target_pairs={{0,8},{4,12},{8,0},{12,4},{1,9},{5,13},{9,1},{13,5},{2,10},{6,14},... | collective-permute-start | bytes 1179656 | tf_op jit(solution)/shard_map/ppermute | solution.py:18

commit v2 on v1

--- a/solution.py
+++ b/solution.py
@@ -10,6 +10,7 @@
 norm_eps = 1e-05
 cos_eps = 1e-06
 glu_alpha = 1.702
+x_parts = 1
 
 
 def swapped(value, axis, bit):
@@ -97,23 +98,27 @@
 
 
 def project_body(count, *refs):
-    tokens_in = refs[:count]
-    own, core_own, near, far, core_near, core_far, hidden_out, rows = refs[count:]
-    tokens, half_depth = tokens_in[0].shape[0], near.shape[0]
-    width = own.shape[1]
-    for block in range(count):
-        rows[block * tokens : (block + 1) * tokens, :] = tokens_in[block][...]
+    tokens_in, (own, core_own), parts = refs[:count], refs[count : count + 2], refs[count + 2 : -2]
+    hidden_out, rows = refs[-2:]
+    step, width = parts[0].shape
+    start = 0
+    for block in tokens_in:
+        rows[start : start + block.shape[0], :] = block[...]
+        start += block.shape[0]
     spot = lax.axis_index("fsdp")
     on_gate = spot < 2
     group = lax.axis_index("groups")
-    near_depth = pl.ds(pl.multiple_of(group * half_depth, half_depth), half_depth)
-    far_depth = pl.ds(pl.multiple_of((1 - group) * half_depth, half_depth), half_depth)
-    for mine, first, second, hidden_block in (
-        (own, near, far, spot % 2),
-        (core_own, core_near, core_far, 1 - spot % 2),
+    depths = [
+        pl.ds(pl.multiple_of((half * x_parts + part) * step, step), step)
+        for half in (group, 1 - group)
+        for part in range(x_parts)
+    ]
+    for mine, theirs, hidden_block in (
+        (own, parts[: 2 * x_parts], spot % 2),
+        (core_own, parts[2 * x_parts :], 1 - spot % 2),
     ):
         here = dot(rows[...], mine[...])
-        there = dot(rows[:, near_depth], first[...]) + dot(rows[:, far_depth], second[...])
+        there = sum(dot(rows[:, depth], part[...]) for depth, part in zip(depths, theirs))
         gate_part = jnp.where(on_gate, here, there)
         up_part = jnp.where(on_gate, there, here)
         columns = pl.ds(pl.multiple_of(hidden_block * width, width), width)
@@ -123,8 +128,8 @@
 
 
 def project(blocks, panels):
-    tokens, features = blocks[0].shape
-    rows = len(blocks) * tokens
+    features = blocks[0].shape[1]
+    rows = sum(block.shape[0] for block in blocks)
     hidden = 2 * panels[0].shape[1]
     return kernel_call(
         functools.partial(project_body, len(blocks)),
@@ -135,26 +140,25 @@
     )(*blocks, *panels)
 
 
-def lower_body(count, hidden, *refs):
+def lower_body(hidden, *refs):
     panels, outs = refs[:4], refs[4:]
-    tokens, width = outs[0].shape[0], panels[0].shape[1]
+    width = panels[0].shape[1]
     spot = lax.axis_index("fsdp")
     for panel, source in zip(panels, (spot, spot ^ 1, spot ^ 2, spot ^ 3)):
         part = dot(hidden[...], panel[...])
         columns = pl.ds(pl.multiple_of(source * width, width), width)
-        for block in range(count):
-            outs[block][:, columns] = part[block * tokens : (block + 1) * tokens].astype(
-                outs[block].dtype
-            )
-
-
-def lower(hidden, panels, kinds):
-    count = len(kinds)
-    tokens = hidden.shape[0] // count
+        start = 0
+        for out in outs:
+            stop = start + out.shape[0]
+            out[:, columns] = part[start:stop].astype(out.dtype)
+            start = stop
+
+
+def lower(hidden, panels, pieces):
     features = 4 * panels[0].shape[1]
     return kernel_call(
-        functools.partial(lower_body, count),
-        tuple(jax.ShapeDtypeStruct((tokens, features), kind) for kind in kinds),
+        lower_body,
+        tuple(jax.ShapeDtypeStruct((rows, features), kind) for rows, kind in pieces),
         (),
         2 * hidden.shape[0] * hidden.shape[1] * features,
         2 * hidden.shape[1] * features + 4 * hidden.shape[0] * features,
@@ -182,36 +186,40 @@
 
 def dense_shards(layer_in, attn_out, norm_gain, expert_ids, gate_weights, w_gate_up, w_down):
     tokens, features = layer_in.shape
-    own_up, own_down = w_gate_up[0], w_down[0]
-    half_depth = features // 2
-    group = lax.axis_index("groups")
-    first_half = lax.dynamic_slice_in_dim(own_up, group * half_depth, half_depth, 0)
-    near = swapped(first_half, "fsdp", 1)
-    x_down = swapped(own_down, "fsdp", 1)
-    far = swapped(near, "groups", 0)
-    core_up, core_down = swapped(own_up, "fsdp", 0), swapped(own_down, "fsdp", 0)
-    core_near, core_far = swapped(near, "fsdp", 0), swapped(far, "fsdp", 0)
-    core_x_down = swapped(x_down, "fsdp", 0)
-    up_panels = (own_up, core_up, near, far, core_near, core_far)
-    down_panels = (own_down, core_down, x_down, core_x_down)
-
     inputs = layer_in.astype(jnp.float32)
     residual = inputs + attn_out.astype(jnp.float32)
     mean_square = jnp.mean(residual * residual, axis=-1, keepdims=True)
     normed = (residual * lax.rsqrt(mean_square + norm_eps) * norm_gain[None, :]).astype(
         jnp.bfloat16
     )
+    own_up, own_down = w_gate_up[0], w_down[0]
+    step = features // (2 * x_parts)
+    first_row = lax.axis_index("groups") * (features // 2)
+    piece0 = lax.dynamic_slice_in_dim(own_up, first_row + 0 * step, step, 0)
     two = swapped(normed, "ep", 1)
     one = swapped(normed, "ep", 0)
-    three = swapped(two, "ep", 0)
-    early = project((normed, one, two), up_panels)
-    kept, sent_one, kept_two = lower(
-        early, down_panels, (jnp.float32, jnp.bfloat16, jnp.float32)
-    )
-    (sent_three,) = lower(project((three,), up_panels), down_panels, (jnp.bfloat16,))
-    got_two = swapped(sent_three, "ep", 0)
-    joined = (kept_two + got_two.astype(jnp.float32)).astype(jnp.bfloat16)
-    other = swapped(joined, "ep", 1)
+    tied_three, *_ = lax.optimization_barrier((two, one))
+    three = swapped(tied_three, "ep", 0)
+    near0 = swapped(piece0, "fsdp", 1)
+    far0 = swapped(near0, "groups", 0)
+    cnear0 = swapped(near0, "fsdp", 0)
+    cfar0 = swapped(far0, "fsdp", 0)
+    x_down = swapped(own_down, "fsdp", 1)
+    tied_core_up, *_ = lax.optimization_barrier((own_up, near0))
+    core_up = swapped(tied_core_up, "fsdp", 0)
+    tied_core_down, *_ = lax.optimization_barrier((own_down, near0))
+    core_down = swapped(tied_core_down, "fsdp", 0)
+    core_x_down = swapped(x_down, "fsdp", 0)
+    up_panels = (own_up, core_up, near0, far0, cnear0, cfar0)
+    down_panels = (own_down, core_down, x_down, core_x_down)
+    hidden = project((three,), up_panels)
+    (sent_three,) = lower(hidden, down_panels, ((tokens, jnp.bfloat16),))
+    early = project((two, normed, one), up_panels)
+    kept_two, kept, sent_one = lower(
+        early, down_panels, tuple((tokens, kind) for kind in (jnp.float32, jnp.float32, jnp.bfloat16))
+    )
+    got = swapped(sent_three, "ep", 0).astype(jnp.float32)
+    other = swapped((kept_two + got).astype(jnp.bfloat16), "ep", 1)
     partner = swapped(sent_one, "ep", 0)
     layer_out, similarity = kernel_call(
         finish_body,

time: 77.5 us -> 71.6 us (0.924)
  waiting for transfers between devices: 50.3 us -> 44.6 us
    ppermute x14, waiting for transfers between devices: 50.3 us -> 44.6 us  [swapped(): return lax.ppermute(value, axis, pairs)]
  transfers between devices with their start and end apart: 14 -> 14, of which waited for: 9 -> 10; matrix products, arithmetic and copies ran while one was open for 1% -> 1% of each run, Pallas kernels for 7% -> 7%
where the time goes in v2:
time: 71.6 us; the launch traced here: 71.4 us
  waiting for transfers between devices  44.6 us (62%)
  starting transfers between devices  17.3 us (24%)
  Pallas kernels  6.86 us (10%)
  local copies, waits for them, and re-layouts  1.46 us (2%)
  between operations  0.76 us (1%)
    ppermute x14, waiting for transfers between devices, swapped(): return lax.ppermute(value, axis, pairs)  44.6 us
    ppermute x14, starting transfers between devices, swapped(): return lax.ppermute(value, axis, pairs)  17.3 us
    pallas_call x2, Pallas kernels, project(): kernel_call(functools.partial(project_body, len(blocks)), jax.ShapeDtypeS...  3.7 us
    pallas_call x2, Pallas kernels, lower(): kernel_call(lower_body, tuple((jax.ShapeDtypeStruct((rows, features), kin...  1.95 us
  transfers between devices with their start and end apart: 14, of which 10 were waited for; matrix products, arithmetic and copies ran while one was open for 1% of the time, Pallas kernels for 7%

profile of v2, /device:TPU:0, one launch (start us, length us, event | category | flops | bytes accessed | tf_op | source)
XLA Modules:
  0.0 71.4 jit_solution(10315686501562322264)
XLA Ops:
  0.7 1.2 %dynamic-slice_bitcast_fusion = bf16[768,384]{1,0:T(8,128)(2,1)S(1)} fusion(bf16[1,1536,384]{2,1,0:T(8,128)(2,1)} %param.12, s32[]{:T(128)S(6)} %select_n.3), kind=kLoop, calls=%fused_computation.4 | loop fusion | bytes 1179652 | tf_op jit(solution)/shard_map/dynamic_slice | solution.py:198
  1.9 0.0 copy-start.3
  1.9 3.0 %collective-permute-start.2 = (bf16[768,384]{1,0:T(8,128)(2,1)S(1)}, bf16[768,384]{1,0:T(8,128)(2,1)S(1)}, u32[]{:S(2)}, u32[]{:S(2)}) collective-permute-start(bf16[768,384]{1,0:T(8,128)(2,1)S(1)} %dynamic-slice_bitcast_fusion), channel_id=1, source_target_pairs={{0,2},{1,3},{2,0},{3,1},{4,6},{5,7},{6,4},{7,5},{8,10},{9,11},{10,... | collective-permute-start | bytes 1769480 | tf_op jit(solution)/shard_map/ppermute | solution.py:19
  4.9 0.2 multiply_reduce_fusion
  5.1 0.2 multiply_convert_fusion.refs_1_
  5.3 2.7 %collective-permute-start = (bf16[128,1536]{1,0:T(8,128)(2,1)S(1)}, bf16[128,1536]{1,0:T(8,128)(2,1)S(1)}, u32[]{:S(2)}, u32[]{:S(2)}) collective-permute-start(bf16[128,1536]{1,0:T(8,128)(2,1)S(1)} %multiply_convert_fusion.refs_1_), channel_id=1, source_target_pairs={{0,8},{4,12},{8,0},{12,4},{1,9},{5,13},{9,1},{13,5},{2,10},{6,14},... | collective-permute-start | bytes 1179656 | tf_op jit(solution)/shard_map/ppermute | solution.py:19
  7.9 1.6 %collective-permute-start.1 = (bf16[128,1536]{1,0:T(8,128)(2,1)S(1)}, bf16[128,1536]{1,0:T(8,128)(2,1)S(1)}, u32[]{:S(2)}, u32[]{:S(2)}) collective-permute-start(bf16[128,1536]{1,0:T(8,128)(2,1)S(1)} %multiply_convert_fusion.refs_1_), channel_id=1, source_target_pairs={{0,4},{4,0},{8,12},{12,8},{1,5},{5,1},{9,13},{13,9},{2,6},{6,2},{1... | collective-permute-start | bytes 1179656 | tf_op jit(solution)/shard_map/ppermute | solution.py:19
  9.5 8.7 %collective-permute-done.2.refs_5_.refs_3_ = bf16[768,384]{1,0:T(8,128)(2,1)S(1)} collective-permute-done((bf16[768,384]{1,0:T(8,128)(2,1)S(1)}, bf16[768,384]{1,0:T(8,128)(2,1)S(1)}, u32[]{:S(2)}, u32[]{:S(2)}) %collective-permute-start.2) | collective-permute-done | bytes 589856 | tf_op jit(solution)/shard_map/ppermute | solution.py:19
  18.2 1.8 %collective-permute-start.4 = (bf16[768,384]{1,0:T(8,128)(2,1)S(1)}, bf16[768,384]{1,0:T(8,128)(2,1)S(1)}, u32[]{:S(2)}, u32[]{:S(2)}) collective-permute-start(bf16[768,384]{1,0:T(8,128)(2,1)S(1)} %collective-permute-done.2.refs_5_.refs_3_), channel_id=1, source_target_pairs={{0,16},{16,0},{1,17},{17,1},{2,18},{18,2},{3,19},{19,3},{4,20},{20... | collective-permute-start | bytes 1769480 | tf_op jit(solution)/shard_map/ppermute | solution.py:19
  20.0 1.6 %collective-permute-start.8 = (bf16[768,384]{1,0:T(8,128)(2,1)S(1)}, bf16[768,384]{1,0:T(8,128)(2,1)S(1)}, u32[]{:S(2)}, u32[]{:S(2)}) collective-permute-start(bf16[768,384]{1,0:T(8,128)(2,1)S(1)} %bitcast.8), channel_id=1, source_target_pairs={{0,2},{1,3},{2,0},{3,1},{4,6},{5,7},{6,4},{7,5},{8,10},{9,11},{10,... | collective-permute-start | bytes 1769480 | tf_op jit(solution)/shard_map/ppermute | solution.py:19
  21.6 3.8 %collective-permute-done.refs_0_ = bf16[128,1536]{1,0:T(8,128)(2,1)S(1)} collective-permute-done((bf16[128,1536]{1,0:T(8,128)(2,1)S(1)}, bf16[128,1536]{1,0:T(8,128)(2,1)S(1)}, u32[]{:S(2)}, u32[]{:S(2)}) %collective-permute-start) | collective-permute-done | bytes 393248 | tf_op jit(solution)/shard_map/ppermute | solution.py:19
  25.4 0.2 collective-permute-done.1.refs_2_
  25.6 1.4 %collective-permute-start.11 = (bf16[128,1536]{1,0:T(8,128)(2,1)S(1)}, bf16[128,1536]{1,0:T(8,128)(2,1)S(1)}, u32[]{:S(2)}, u32[]{:S(2)}) collective-permute-start(bf16[128,1536]{1,0:T(8,128)(2,1)S(1)} %collective-permute-done.refs_0_), channel_id=1, source_target_pairs={{0,4},{4,0},{8,12},{12,8},{1,5},{5,1},{9,13},{13,9},{2,6},{6,2},{1... | collective-permute-start | bytes 1179656 | tf_op jit(solution)/shard_map/ppermute | solution.py:19
  27.0 5.7 %collective-permute-done.4.refs_6_.refs_4_ = bf16[768,384]{1,0:T(8,128)(2,1)S(1)} collective-permute-done((bf16[768,384]{1,0:T(8,128)(2,1)S(1)}, bf16[768,384]{1,0:T(8,128)(2,1)S(1)}, u32[]{:S(2)}, u32[]{:S(2)}) %collective-permute-start.4) | collective-permute-done | bytes 589856 | tf_op jit(solution)/shard_map/ppermute | solution.py:19
  32.7 3.0 %collective-permute-done.8.refs_2_ = bf16[768,384]{1,0:T(8,128)(2,1)S(1)} collective-permute-done((bf16[768,384]{1,0:T(8,128)(2,1)S(1)}, bf16[768,384]{1,0:T(8,128)(2,1)S(1)}, u32[]{:S(2)}, u32[]{:S(2)}) %collective-permute-start.8) | collective-permute-done | bytes 589856 | tf_op jit(solution)/shard_map/ppermute | solution.py:19
  35.7 0.5 collective-permute-start.9
  36.3 1.0 %shard_map.88.hidden = bf16[128,768]{1,0:T(8,128)(2,1)S(1)} custom-call(bf16[128,1536]{1,0:T(8,128)(2,1)S(1)} %collective-permute-done.11.refs_0_, bf16[1536,384]{1,0:T(8,128)(2,1)S(1)} %bitcast.6, bf16[1536,384]{1,0:T(8,128)(2,1)S(1)} %collective-permute-done.3.refs_4_.refs_2_, bf16[768,384]{1,0:T(8,128)(2,1)S(1)} %collective-permute-done.2.refs_5_.refs_3_, ...), custom_call_target="tpu_custom_call" | custom-call | flops 603979776 | bytes 5308416 | tf_op jit(solution)/shard_map/pallas_call | solution.py:134
  37.3 0.4 collective-permute-done.7.refs_1_
  37.7 0.8 %collective-permute-done.9.refs_3_ = bf16[768,384]{1,0:T(8,128)(2,1)S(1)} collective-permute-done((bf16[768,384]{1,0:T(8,128)(2,1)S(1)}, bf16[768,384]{1,0:T(8,128)(2,1)S(1)}, u32[]{:S(2)}, u32[]{:S(2)}) %collective-permute-start.9) | collective-permute-done | bytes 589856 | tf_op jit(solution)/shard_map/ppermute | solution.py:19
  38.6 0.6 shard_map.89
  39.2 1.6 %collective-permute-start.12 = (bf16[128,1536]{1,0:T(8,128)(2,1)S(1)}, bf16[128,1536]{1,0:T(8,128)(2,1)S(1)}, u32[]{:S(2)}, u32[]{:S(2)}) collective-permute-start(bf16[128,1536]{1,0:T(8,128)(2,1)S(1)} %shard_map.89), channel_id=1, source_target_pairs={{0,4},{4,0},{8,12},{12,8},{1,5},{5,1},{9,13},{13,9},{2,6},{6,2},{1... | collective-permute-start | bytes 1179656 | tf_op jit(solution)/shard_map/ppermute | solution.py:19
  40.8 2.7 %shard_map.86.hidden = bf16[384,768]{1,0:T(8,128)(2,1)S(1)} custom-call(bf16[128,1536]{1,0:T(8,128)(2,1)S(1)} %collective-permute-done.refs_0_, bf16[128,1536]{1,0:T(8,128)(2,1)S(1)} %multiply_convert_fusion.refs_1_, bf16[128,1536]{1,0:T(8,128)(2,1)S(1)} %collective-permute-done.1.refs_2_, bf16[1536,384]{1,0:T(8,128)(2,1)S(1)} %bitcast.7, ...), custom_call_target="tpu_custom_call" | custom-call | flops 1811939328 | bytes 6488064 | tf_op jit(solution)/shard_map/pallas_call | solution.py:134
  43.5 1.4 %shard_map.87 = (f32[128,1536]{1,0:T(8,128)S(1)}, f32[128,1536]{1,0:T(8,128)S(1)}, bf16[128,1536]{1,0:T(8,128)(2,1)S(1)}) custom-call(bf16[384,768]{1,0:T(8,128)(2,1)S(1)} %shard_map.86.hidden, bf16[768,384]{1,0:T(8,128)(2,1)S(1)} %bitcast.11, bf16[768,384]{1,0:T(8,128)(2,1)S(1)} %collective-permute-done.7.refs_1_, ...), custom_call_target="tpu_custom_call" | custom-call | flops 905969664 | bytes 4718592 | tf_op jit(solution)/shard_map/pallas_call | solution.py:159
  44.9 0.5 collective-permute-start.10
  45.4 5.8 %collective-permute-done.12 = bf16[128,1536]{1,0:T(8,128)(2,1)S(1)} collective-permute-done((bf16[128,1536]{1,0:T(8,128)(2,1)S(1)}, bf16[128,1536]{1,0:T(8,128)(2,1)S(1)}, u32[]{:S(2)}, u32[]{:S(2)}) %collective-permute-start.12) | collective-permute-done | bytes 393248 | tf_op jit(solution)/shard_map/ppermute | solution.py:19
  51.2 0.1 add_convert_fusion
  51.3 2.6 %collective-permute-start.13 = (bf16[128,1536]{1,0:T(8,128)(2,1)S(1)}, bf16[128,1536]{1,0:T(8,128)(2,1)S(1)}, u32[]{:S(2)}, u32[]{:S(2)}) collective-permute-start(bf16[128,1536]{1,0:T(8,128)(2,1)S(1)} %add_convert_fusion), channel_id=1, source_target_pairs={{0,8},{4,12},{8,0},{12,4},{1,9},{5,13},{9,1},{13,5},{2,10},{6,14},... | collective-permute-start | bytes 1179656 | tf_op jit(solution)/shard_map/ppermute | solution.py:19
  53.9 0.1 copy.10.weights
  54.0 0.1 copy.9.ids
  54.1 12.2 %collective-permute-done.10.partner = bf16[128,1536]{1,0:T(8,128)(2,1)S(1)} collective-permute-done((bf16[128,1536]{1,0:T(8,128)(2,1)S(1)}, bf16[128,1536]{1,0:T(8,128)(2,1)S(1)}, u32[]{:S(2)}, u32[]{:S(2)}) %collective-permute-start.10) | collective-permute-done | bytes 393248 | tf_op jit(solution)/shard_map/ppermute | solution.py:19
  66.4 3.8 %collective-permute-done.13.other = bf16[128,1536]{1,0:T(8,128)(2,1)S(1)} collective-permute-done((bf16[128,1536]{1,0:T(8,128)(2,1)S(1)}, bf16[128,1536]{1,0:T(8,128)(2,1)S(1)}, u32[]{:S(2)}, u32[]{:S(2)}) %collective-permute-start.13) | collective-permute-done | bytes 393248 | tf_op jit(solution)/shard_map/ppermute | solution.py:19
  70.2 1.2 %shard_map.90 = (bf16[128,1536]{1,0:T(8,128)(2,1)}, f32[1,128]{1,0:T(1,128)}) custom-call(bf16[128,1536]{1,0:T(8,128)(2,1)S(1)} %copy-done, bf16[128,1536]{1,0:T(8,128)(2,1)S(1)} %copy-done.1, s32[128,2]{1,0:T(8,128)S(1)} %copy.9.ids, f32[128,2]{1,0:T(8,128)S(1)} %copy.10.weights, f32[128,1536]{1,0:T(8,128)S(1)} %get-tuple-element.12.kept, ...), custom_call_target="tpu_custom_call" | custom-call | flops 3932160 | bytes 3145728 | tf_op jit(solution)/shard_map/pallas_call | solution.py:224
  (22 shorter events, 0.1 us)
Async XLA Ops:
  0.6 4.3 %copy-start = (bf16[128,1536]{1,0:T(8,128)(2,1)S(1)}, bf16[128,1536]{1,0:T(8,128)(2,1)}, u32[]{:S(2)}) copy-start(bf16[128,1536]{1,0:T(8,128)(2,1)} %layer_in.1) | copy-start | bytes 1179652
  0.6 4.3 %copy-start.1 = (bf16[128,1536]{1,0:T(8,128)(2,1)S(1)}, bf16[128,1536]{1,0:T(8,128)(2,1)}, u32[]{:S(2)}) copy-start(bf16[128,1536]{1,0:T(8,128)(2,1)} %attn_out.1) | copy-start | bytes 1179652
  0.6 4.5 %copy-start.4 = (f32[1536]{0:T(1024)S(1)}, f32[1536]{0:T(1024)}, u32[]{:S(2)}) copy-start(f32[1536]{0:T(1024)} %param.9) | copy-start | bytes 18436
  1.9 18.1 %copy-start.2 = (bf16[1,1536,384]{2,1,0:T(8,128)(2,1)S(1)}, bf16[1,1536,384]{2,1,0:T(8,128)(2,1)}, u32[]{:S(2)}) copy-start(bf16[1,1536,384]{2,1,0:T(8,128)(2,1)} %param.12) | copy-start | bytes 3538948
  1.9 18.1 %copy-start.3 = (bf16[1,768,384]{2,1,0:T(8,128)(2,1)S(1)}, bf16[1,768,384]{2,1,0:T(8,128)(2,1)}, u32[]{:S(2)}) copy-start(bf16[1,768,384]{2,1,0:T(8,128)(2,1)} %param.13) | copy-start | bytes 1769476
  1.9 16.3 %collective-permute-start.2 = (bf16[768,384]{1,0:T(8,128)(2,1)S(1)}, bf16[768,384]{1,0:T(8,128)(2,1)S(1)}, u32[]{:S(2)}, u32[]{:S(2)}) collective-permute-start(bf16[768,384]{1,0:T(8,128)(2,1)S(1)} %dynamic-slice_bitcast_fusion), channel_id=1, source_target_pairs={{0,2},{1,3},{2,0},{3,1},{4,6},{5,7},{6,4},{7,5},{8,10},{9,11},{10,... | collective-permute-start | bytes 1769480 | tf_op jit(solution)/shard_map/ppermute | solution.py:19
  5.3 20.1 %collective-permute-start = (bf16[128,1536]{1,0:T(8,128)(2,1)S(1)}, bf16[128,1536]{1,0:T(8,128)(2,1)S(1)}, u32[]{:S(2)}, u32[]{:S(2)}) collective-permute-start(bf16[128,1536]{1,0:T(8,128)(2,1)S(1)} %multiply_convert_fusion.refs_1_), channel_id=1, source_target_pairs={{0,8},{4,12},{8,0},{12,4},{1,9},{5,13},{9,1},{13,5},{2,10},{6,14},... | collective-permute-start | bytes 1179656 | tf_op jit(solution)/shard_map/ppermute | solution.py:19
  7.9 17.6 %collective-permute-start.1 = (bf16[128,1536]{1,0:T(8,128)(2,1)S(1)}, bf16[128,1536]{1,0:T(8,128)(2,1)S(1)}, u32[]{:S(2)}, u32[]{:S(2)}) collective-permute-start(bf16[128,1536]{1,0:T(8,128)(2,1)S(1)} %multiply_convert_fusion.refs_1_), channel_id=1, source_target_pairs={{0,4},{4,0},{8,12},{12,8},{1,5},{5,1},{9,13},{13,9},{2,6},{6,2},{1... | collective-permute-start | bytes 1179656 | tf_op jit(solution)/shard_map/ppermute | solution.py:19
  18.2 14.5 %collective-permute-start.4 = (bf16[768,384]{1,0:T(8,128)(2,1)S(1)}, bf16[768,384]{1,0:T(8,128)(2,1)S(1)}, u32[]{:S(2)}, u32[]{:S(2)}) collective-permute-start(bf16[768,384]{1,0:T(8,128)(2,1)S(1)} %collective-permute-done.2.refs_5_.refs_3_), channel_id=1, source_target_pairs={{0,16},{16,0},{1,17},{17,1},{2,18},{18,2},{3,19},{19,3},{4,20},{20... | collective-permute-start | bytes 1769480 | tf_op jit(solution)/shard_map/ppermute | solution.py:19
  20.0 16.3 %collective-permute-start.3 = (bf16[1536,384]{1,0:T(8,128)(2,1)S(1)}, bf16[1536,384]{1,0:T(8,128)(2,1)S(1)}, u32[]{:S(2)}, u32[]{:S(2)}) collective-permute-start(bf16[1536,384]{1,0:T(8,128)(2,1)S(1)} %bitcast.5), channel_id=1, source_target_pairs={{0,1},{1,0},{2,3},{3,2},{4,5},{5,4},{6,7},{7,6},{8,9},{9,8},{10,11... | collective-permute-start | bytes 3538952 | tf_op jit(solution)/shard_map/ppermute | solution.py:19
  20.0 15.7 %collective-permute-start.8 = (bf16[768,384]{1,0:T(8,128)(2,1)S(1)}, bf16[768,384]{1,0:T(8,128)(2,1)S(1)}, u32[]{:S(2)}, u32[]{:S(2)}) collective-permute-start(bf16[768,384]{1,0:T(8,128)(2,1)S(1)} %bitcast.8), channel_id=1, source_target_pairs={{0,2},{1,3},{2,0},{3,1},{4,6},{5,7},{6,4},{7,5},{8,10},{9,11},{10,... | collective-permute-start | bytes 1769480 | tf_op jit(solution)/shard_map/ppermute | solution.py:19
  25.6 10.2 %collective-permute-start.11 = (bf16[128,1536]{1,0:T(8,128)(2,1)S(1)}, bf16[128,1536]{1,0:T(8,128)(2,1)S(1)}, u32[]{:S(2)}, u32[]{:S(2)}) collective-permute-start(bf16[128,1536]{1,0:T(8,128)(2,1)S(1)} %collective-permute-done.refs_0_), channel_id=1, source_target_pairs={{0,4},{4,0},{8,12},{12,8},{1,5},{5,1},{9,13},{13,9},{2,6},{6,2},{1... | collective-permute-start | bytes 1179656 | tf_op jit(solution)/shard_map/ppermute | solution.py:19
  27.0 9.3 %collective-permute-start.5 = (bf16[768,384]{1,0:T(8,128)(2,1)S(1)}, bf16[768,384]{1,0:T(8,128)(2,1)S(1)}, u32[]{:S(2)}, u32[]{:S(2)}) collective-permute-start(bf16[768,384]{1,0:T(8,128)(2,1)S(1)} %collective-permute-done.2.refs_5_.refs_3_), channel_id=1, source_target_pairs={{0,1},{1,0},{2,3},{3,2},{4,5},{5,4},{6,7},{7,6},{8,9},{9,8},{10,11... | collective-permute-start | bytes 1769480 | tf_op jit(solution)/shard_map/ppermute | solution.py:19
  32.7 3.5 %collective-permute-start.6 = (bf16[768,384]{1,0:T(8,128)(2,1)S(1)}, bf16[768,384]{1,0:T(8,128)(2,1)S(1)}, u32[]{:S(2)}, u32[]{:S(2)}) collective-permute-start(bf16[768,384]{1,0:T(8,128)(2,1)S(1)} %collective-permute-done.4.refs_6_.refs_4_), channel_id=1, source_target_pairs={{0,1},{1,0},{2,3},{3,2},{4,5},{5,4},{6,7},{7,6},{8,9},{9,8},{10,11... | collective-permute-start | bytes 1769480 | tf_op jit(solution)/shard_map/ppermute | solution.py:19
  35.7 2.0 %collective-permute-start.7 = (bf16[768,384]{1,0:T(8,128)(2,1)S(1)}, bf16[768,384]{1,0:T(8,128)(2,1)S(1)}, u32[]{:S(2)}, u32[]{:S(2)}) collective-permute-start(bf16[768,384]{1,0:T(8,128)(2,1)S(1)} %bitcast.9), channel_id=1, source_target_pairs={{0,1},{1,0},{2,3},{3,2},{4,5},{5,4},{6,7},{7,6},{8,9},{9,8},{10,11... | collective-permute-start | bytes 1769480 | tf_op jit(solution)/shard_map/ppermute | solution.py:19
  35.7 2.8 %collective-permute-start.9 = (bf16[768,384]{1,0:T(8,128)(2,1)S(1)}, bf16[768,384]{1,0:T(8,128)(2,1)S(1)}, u32[]{:S(2)}, u32[]{:S(2)}) collective-permute-start(bf16[768,384]{1,0:T(8,128)(2,1)S(1)} %collective-permute-done.8.refs_2_), channel_id=1, source_target_pairs={{0,1},{1,0},{2,3},{3,2},{4,5},{5,4},{6,7},{7,6},{8,9},{9,8},{10,11... | collective-permute-start | bytes 1769480 | tf_op jit(solution)/shard_map/ppermute | solution.py:19
  39.2 12.0 %collective-permute-start.12 = (bf16[128,1536]{1,0:T(8,128)(2,1)S(1)}, bf16[128,1536]{1,0:T(8,128)(2,1)S(1)}, u32[]{:S(2)}, u32[]{:S(2)}) collective-permute-start(bf16[128,1536]{1,0:T(8,128)(2,1)S(1)} %shard_map.89), channel_id=1, source_target_pairs={{0,4},{4,0},{8,12},{12,8},{1,5},{5,1},{9,13},{13,9},{2,6},{6,2},{1... | collective-permute-start | bytes 1179656 | tf_op jit(solution)/shard_map/ppermute | solution.py:19
  44.9 9.0 %copy-start.5 = (f32[128,2]{0,1:T(2,128)S(1)}, f32[128,2]{0,1:T(2,128)}, u32[]{:S(2)}) copy-start(f32[128,2]{0,1:T(2,128)} %param.11) | copy-start | bytes 3076
  44.9 9.1 %copy-start.6 = (s32[128,2]{0,1:T(2,128)S(1)}, s32[128,2]{0,1:T(2,128)}, u32[]{:S(2)}) copy-start(s32[128,2]{0,1:T(2,128)} %param.10) | copy-start | bytes 3076
  44.9 21.5 %collective-permute-start.10 = (bf16[128,1536]{1,0:T(8,128)(2,1)S(1)}, bf16[128,1536]{1,0:T(8,128)(2,1)S(1)}, u32[]{:S(2)}, u32[]{:S(2)}) collective-permute-start(bf16[128,1536]{1,0:T(8,128)(2,1)S(1)} %get-tuple-element.13), channel_id=1, source_target_pairs={{0,4},{4,0},{8,12},{12,8},{1,5},{5,1},{9,13},{13,9},{2,6},{6,2},{1... | collective-permute-start | bytes 1179656 | tf_op jit(solution)/shard_map/ppermute | solution.py:19
  51.3 19.0 %collective-permute-start.13 = (bf16[128,1536]{1,0:T(8,128)(2,1)S(1)}, bf16[128,1536]{1,0:T(8,128)(2,1)S(1)}, u32[]{:S(2)}, u32[]{:S(2)}) collective-permute-start(bf16[128,1536]{1,0:T(8,128)(2,1)S(1)} %add_convert_fusion), channel_id=1, source_target_pairs={{0,8},{4,12},{8,0},{12,4},{1,9},{5,13},{9,1},{13,5},{2,10},{6,14},... | collective-permute-start | bytes 1179656 | tf_op jit(solution)/shard_map/ppermute | solution.py:19

commit v3 on v2

--- a/solution.py
+++ b/solution.py
@@ -91,6 +91,19 @@
         compiler_params=pltpu.CompilerParams(vmem_limit_bytes=40 * 2**20),
         cost_estimate=pl.CostEstimate(flops=flops, bytes_accessed=moved, transcendentals=0),
     )
+
+
+def after_body(value, *refs):
+    refs[-1][...] = value[...]
+
+
+def after(value, *others, flops=0):
+    return kernel_call(
+        after_body,
+        jax.ShapeDtypeStruct(value.shape, value.dtype),
+        flops=flops,
+        moved=4 * value.size,
+    )(value, *others)
 
 
 def dot(left, right):
@@ -165,7 +178,8 @@
     )(hidden, *panels)
 
 
-def finish_body(layer_in, attn_out, ids, weights, kept, partner, other, layer_out, similarity):
+def finish_body(layer_in, attn_out, ids, weights, kept, partner, *refs):
+    others, (layer_out, similarity) = refs[:-2], refs[-2:]
     inputs = layer_in[...].astype(jnp.float32)
     residual = inputs + attn_out[...].astype(jnp.float32)
     mine = (kept[...] + partner[...].astype(jnp.float32)).astype(jnp.bfloat16).astype(jnp.float32)
@@ -173,7 +187,8 @@
     named = ids[...] == own_expert
     own_gate = jnp.sum(jnp.where(named, weights[...], 0.0), axis=1, keepdims=True)
     other_gate = jnp.sum(jnp.where(named, 0.0, weights[...]), axis=1, keepdims=True)
-    updated = residual + (own_gate * mine + other_gate * other[...].astype(jnp.float32))
+    other = jnp.concatenate([part[...] for part in others], axis=0).astype(jnp.float32)
+    updated = residual + (own_gate * mine + other_gate * other)
     layer_out[...] = updated.astype(jnp.bfloat16)
     value = (
         jnp.sum(inputs * updated, axis=-1, keepdims=True)
@@ -199,27 +214,33 @@
     two = swapped(normed, "ep", 1)
     one = swapped(normed, "ep", 0)
     tied_three, *_ = lax.optimization_barrier((two, one))
-    three = swapped(tied_three, "ep", 0)
+    src_three = after(tied_three, flops=int(3e9))
+    three = swapped(src_three, "ep", 0)
     near0 = swapped(piece0, "fsdp", 1)
     far0 = swapped(near0, "groups", 0)
     cnear0 = swapped(near0, "fsdp", 0)
     cfar0 = swapped(far0, "fsdp", 0)
     x_down = swapped(own_down, "fsdp", 1)
-    tied_core_up, *_ = lax.optimization_barrier((own_up, near0))
-    core_up = swapped(tied_core_up, "fsdp", 0)
-    tied_core_down, *_ = lax.optimization_barrier((own_down, near0))
-    core_down = swapped(tied_core_down, "fsdp", 0)
-    core_x_down = swapped(x_down, "fsdp", 0)
+    src_core_up = after(own_up, flops=int(2e9))
+    core_up = swapped(src_core_up, "fsdp", 0)
+    core_down = swapped(own_down, "fsdp", 0)
+    src_core_x_down = after(x_down, flops=int(4e9))
+    core_x_down = swapped(src_core_x_down, "fsdp", 0)
     up_panels = (own_up, core_up, near0, far0, cnear0, cfar0)
     down_panels = (own_down, core_down, x_down, core_x_down)
+    half = tokens // 2
+    wide, narrow = jnp.float32, jnp.bfloat16
     hidden = project((three,), up_panels)
-    (sent_three,) = lower(hidden, down_panels, ((tokens, jnp.bfloat16),))
+    sent_a, sent_b = lower(hidden, down_panels, ((half, narrow),) * 2)
     early = project((two, normed, one), up_panels)
-    kept_two, kept, sent_one = lower(
-        early, down_panels, tuple((tokens, kind) for kind in (jnp.float32, jnp.float32, jnp.bfloat16))
-    )
-    got = swapped(sent_three, "ep", 0).astype(jnp.float32)
-    other = swapped((kept_two + got).astype(jnp.bfloat16), "ep", 1)
+    kept_a, kept_b, kept, sent_one = lower(
+        early, down_panels, ((half, wide), (half, wide), (tokens, wide), (tokens, narrow))
+    )
+    got_a, got_b = swapped(sent_a, "ep", 0), swapped(sent_b, "ep", 0)
+    joined_a = (kept_a + got_a.astype(jnp.float32)).astype(jnp.bfloat16)
+    joined_b = (kept_b + got_b.astype(jnp.float32)).astype(jnp.bfloat16)
+    other_a, other_b = swapped(joined_a, "ep", 1), swapped(joined_b, "ep", 1)
+    sent_one = after(sent_one, got_b)
     partner = swapped(sent_one, "ep", 0)
     layer_out, similarity = kernel_call(
         finish_body,
@@ -230,7 +251,7 @@
         (),
         20 * tokens * features,
         16 * tokens * features,
-    )(layer_in, attn_out, expert_ids, gate_weights, kept, partner, other)
+    )(layer_in, attn_out, expert_ids, gate_weights, kept, partner, other_a, other_b)
     return layer_out, similarity.reshape(tokens)
 
 

time: 71.6 us -> 67 us (0.936)
  waiting for transfers between devices: 44.6 us -> 40.8 us
  starting transfers between devices: 17.3 us -> 16.3 us
    ppermute x14 -> x16, waiting for transfers between devices: 44.6 us -> 40.8 us  [swapped(): return lax.ppermute(value, axis, pairs)]
    ppermute x14 -> x16, starting transfers between devices: 17.3 us -> 16.3 us  [swapped(): return lax.ppermute(value, axis, pairs)]
  transfers between devices with their start and end apart: 14 -> 16, of which waited for: 10 -> 12; matrix products, arithmetic and copies ran while one was open for 1% -> 1% of each run, Pallas kernels for 7% -> 8%
where the time goes in v3:
time: 67 us; the launch traced here: 66.9 us
  waiting for transfers between devices  40.8 us (61%)
  starting transfers between devices  16.3 us (24%)
  Pallas kernels  7.06 us (11%)
  local copies, waits for them, and re-layouts  1.45 us (2%)
  between operations  0.79 us (1%)
    ppermute x16, waiting for transfers between devices, swapped(): return lax.ppermute(value, axis, pairs)  40.8 us
    ppermute x16, starting transfers between devices, swapped(): return lax.ppermute(value, axis, pairs)  16.3 us
    pallas_call x2, Pallas kernels, project(): kernel_call(functools.partial(project_body, len(blocks)), jax.ShapeDtypeS...  3.7 us
    pallas_call x2, Pallas kernels, lower(): kernel_call(lower_body, tuple((jax.ShapeDtypeStruct((rows, features), kin...  1.95 us
  transfers between devices with their start and end apart: 16, of which 12 were waited for; matrix products, arithmetic and copies ran while one was open for 1% of the time, Pallas kernels for 8%

profile of v3, /device:TPU:0, one launch (start us, length us, event | category | flops | bytes accessed | tf_op | source)
XLA Modules:
  0.0 66.9 jit_solution(11402848362136270926)
XLA Ops:
  0.7 1.2 %dynamic-slice_bitcast_fusion = bf16[768,384]{1,0:T(8,128)(2,1)S(1)} fusion(bf16[1,1536,384]{2,1,0:T(8,128)(2,1)} %param.12, s32[]{:T(128)S(6)} %select_n.3), kind=kLoop, calls=%fused_computation.3 | loop fusion | bytes 1179652 | tf_op jit(solution)/shard_map/dynamic_slice | solution.py:213
  1.9 3.0 %collective-permute-start.3 = (bf16[768,384]{1,0:T(8,128)(2,1)S(1)}, bf16[768,384]{1,0:T(8,128)(2,1)S(1)}, u32[]{:S(2)}, u32[]{:S(2)}) collective-permute-start(bf16[768,384]{1,0:T(8,128)(2,1)S(1)} %dynamic-slice_bitcast_fusion), channel_id=1, source_target_pairs={{0,2},{1,3},{2,0},{3,1},{4,6},{5,7},{6,4},{7,5},{8,10},{9,11},{10,... | collective-permute-start | bytes 1769480 | tf_op jit(solution)/shard_map/ppermute | solution.py:19
  4.9 0.2 multiply_reduce_fusion
  5.1 0.2 multiply_convert_fusion.refs_1_
  5.3 1.6 %collective-permute-start.1 = (bf16[128,1536]{1,0:T(8,128)(2,1)S(1)}, bf16[128,1536]{1,0:T(8,128)(2,1)S(1)}, u32[]{:S(2)}, u32[]{:S(2)}) collective-permute-start(bf16[128,1536]{1,0:T(8,128)(2,1)S(1)} %multiply_convert_fusion.refs_1_), channel_id=1, source_target_pairs={{0,4},{4,0},{8,12},{12,8},{1,5},{5,1},{9,13},{13,9},{2,6},{6,2},{1... | collective-permute-start | bytes 1179656 | tf_op jit(solution)/shard_map/ppermute | solution.py:19
  6.9 2.6 %collective-permute-start = (bf16[128,1536]{1,0:T(8,128)(2,1)S(1)}, bf16[128,1536]{1,0:T(8,128)(2,1)S(1)}, u32[]{:S(2)}, u32[]{:S(2)}) collective-permute-start(bf16[128,1536]{1,0:T(8,128)(2,1)S(1)} %multiply_convert_fusion.refs_1_), channel_id=1, source_target_pairs={{0,8},{4,12},{8,0},{12,4},{1,9},{5,13},{9,1},{13,5},{2,10},{6,14},... | collective-permute-start | bytes 1179656 | tf_op jit(solution)/shard_map/ppermute | solution.py:19
  9.5 0.5 collective-permute-start.8
  10.1 9.0 %collective-permute-done.3.refs_5_.refs_3_ = bf16[768,384]{1,0:T(8,128)(2,1)S(1)} collective-permute-done((bf16[768,384]{1,0:T(8,128)(2,1)S(1)}, bf16[768,384]{1,0:T(8,128)(2,1)S(1)}, u32[]{:S(2)}, u32[]{:S(2)}) %collective-permute-start.3) | collective-permute-done | bytes 589856 | tf_op jit(solution)/shard_map/ppermute | solution.py:19
  19.0 2.1 %collective-permute-start.4 = (bf16[768,384]{1,0:T(8,128)(2,1)S(1)}, bf16[768,384]{1,0:T(8,128)(2,1)S(1)}, u32[]{:S(2)}, u32[]{:S(2)}) collective-permute-start(bf16[768,384]{1,0:T(8,128)(2,1)S(1)} %collective-permute-done.3.refs_5_.refs_3_), channel_id=1, source_target_pairs={{0,16},{16,0},{1,17},{17,1},{2,18},{18,2},{3,19},{19,3},{4,20},{20... | collective-permute-start | bytes 1769480 | tf_op jit(solution)/shard_map/ppermute | solution.py:19
  21.3 2.9 %collective-permute-done.1.refs_2_ = bf16[128,1536]{1,0:T(8,128)(2,1)S(1)} collective-permute-done((bf16[128,1536]{1,0:T(8,128)(2,1)S(1)}, bf16[128,1536]{1,0:T(8,128)(2,1)S(1)}, u32[]{:S(2)}, u32[]{:S(2)}) %collective-permute-start.1) | collective-permute-done | bytes 393248 | tf_op jit(solution)/shard_map/ppermute | solution.py:19
  24.2 2.4 %collective-permute-done.refs_0_.value = bf16[128,1536]{1,0:T(8,128)(2,1)S(1)} collective-permute-done((bf16[128,1536]{1,0:T(8,128)(2,1)S(1)}, bf16[128,1536]{1,0:T(8,128)(2,1)S(1)}, u32[]{:S(2)}, u32[]{:S(2)}) %collective-permute-start) | collective-permute-done | bytes 393248 | tf_op jit(solution)/shard_map/ppermute | solution.py:19
  26.6 0.5 collective-permute-start.10
  27.1 3.7 %collective-permute-done.8.value.refs_2_ = bf16[768,384]{1,0:T(8,128)(2,1)S(1)} collective-permute-done((bf16[768,384]{1,0:T(8,128)(2,1)S(1)}, bf16[768,384]{1,0:T(8,128)(2,1)S(1)}, u32[]{:S(2)}, u32[]{:S(2)}) %collective-permute-start.8) | collective-permute-done | bytes 589856 | tf_op jit(solution)/shard_map/ppermute | solution.py:19
  30.9 1.9 %collective-permute-done.4.refs_6_.refs_4_ = bf16[768,384]{1,0:T(8,128)(2,1)S(1)} collective-permute-done((bf16[768,384]{1,0:T(8,128)(2,1)S(1)}, bf16[768,384]{1,0:T(8,128)(2,1)S(1)}, u32[]{:S(2)}, u32[]{:S(2)}) %collective-permute-start.4) | collective-permute-done | bytes 589856 | tf_op jit(solution)/shard_map/ppermute | solution.py:19
  32.8 2.2 %collective-permute-done.10.refs_0_ = bf16[128,1536]{1,0:T(8,128)(2,1)S(1)} collective-permute-done((bf16[128,1536]{1,0:T(8,128)(2,1)S(1)}, bf16[128,1536]{1,0:T(8,128)(2,1)S(1)}, u32[]{:S(2)}, u32[]{:S(2)}) %collective-permute-start.10) | collective-permute-done | bytes 393248 | tf_op jit(solution)/shard_map/ppermute | solution.py:19
  35.1 1.0 %shard_map.91.hidden = bf16[128,768]{1,0:T(8,128)(2,1)S(1)} custom-call(bf16[128,1536]{1,0:T(8,128)(2,1)S(1)} %collective-permute-done.10.refs_0_, bf16[1536,384]{1,0:T(8,128)(2,1)S(1)} %bitcast.6, bf16[1536,384]{1,0:T(8,128)(2,1)S(1)} %collective-permute-done.2.refs_4_.refs_2_, bf16[768,384]{1,0:T(8,128)(2,1)S(1)} %collective-permute-done.3.refs_5_.refs_3_, ...), custom_call_target="tpu_custom_call" | custom-call | flops 603979776 | bytes 5308416 | tf_op jit(solution)/shard_map/pallas_call | solution.py:147
  36.1 0.9 %collective-permute-done.9.refs_3_ = bf16[768,384]{1,0:T(8,128)(2,1)S(1)} collective-permute-done((bf16[768,384]{1,0:T(8,128)(2,1)S(1)}, bf16[768,384]{1,0:T(8,128)(2,1)S(1)}, u32[]{:S(2)}, u32[]{:S(2)}) %collective-permute-start.9) | collective-permute-done | bytes 589856 | tf_op jit(solution)/shard_map/ppermute | solution.py:19
  37.0 0.6 shard_map.92
  37.6 1.8 %collective-permute-start.11 = (bf16[64,1536]{1,0:T(8,128)(2,1)S(1)}, bf16[64,1536]{1,0:T(8,128)(2,1)S(1)}, u32[]{:S(2)}, u32[]{:S(2)}) collective-permute-start(bf16[64,1536]{1,0:T(8,128)(2,1)S(1)} %get-tuple-element.14), channel_id=1, source_target_pairs={{0,4},{4,0},{8,12},{12,8},{1,5},{5,1},{9,13},{13,9},{2,6},{6,2},{1... | collective-permute-start | bytes 589832 | tf_op jit(solution)/shard_map/ppermute | solution.py:19
  39.4 0.3 collective-permute-start.13
  39.7 2.7 %shard_map.87.hidden = bf16[384,768]{1,0:T(8,128)(2,1)S(1)} custom-call(bf16[128,1536]{1,0:T(8,128)(2,1)S(1)} %collective-permute-done.refs_0_.value, bf16[128,1536]{1,0:T(8,128)(2,1)S(1)} %multiply_convert_fusion.refs_1_, bf16[128,1536]{1,0:T(8,128)(2,1)S(1)} %collective-permute-done.1.refs_2_, bf16[1536,384]{1,0:T(8,128)(2,1)S(1)} %bitcast.7, ...), custom_call_target="tpu_custom_call" | custom-call | flops 1811939328 | bytes 6488064 | tf_op jit(solution)/shard_map/pallas_call | solution.py:147
  42.4 1.4 %shard_map.89 = (f32[64,1536]{1,0:T(8,128)S(1)}, f32[64,1536]{1,0:T(8,128)S(1)}, f32[128,1536]{1,0:T(8,128)S(1)}, bf16[128,1536]{1,0:T(8,128)(2,1)S(1)}) custom-call(bf16[384,768]{1,0:T(8,128)(2,1)S(1)} %shard_map.87.hidden, bf16[768,384]{1,0:T(8,128)(2,1)S(1)} %bitcast.11, bf16[768,384]{1,0:T(8,128)(2,1)S(1)} %collective-permute-done.7.refs_1_, ...), custom_call_target="tpu_custom_call" | custom-call | flops 905969664 | bytes 4718592 | tf_op jit(solution)/shard_map/pallas_call | solution.py:172
  43.8 1.6 %collective-permute-done.11.refs_0_ = bf16[64,1536]{1,0:T(8,128)(2,1)S(1)} collective-permute-done((bf16[64,1536]{1,0:T(8,128)(2,1)S(1)}, bf16[64,1536]{1,0:T(8,128)(2,1)S(1)}, u32[]{:S(2)}, u32[]{:S(2)}) %collective-permute-start.11) | collective-permute-done | bytes 196640 | tf_op jit(solution)/shard_map/ppermute | solution.py:19
  45.5 1.7 %collective-permute-start.15 = (bf16[64,1536]{1,0:T(8,128)(2,1)S(1)}, bf16[64,1536]{1,0:T(8,128)(2,1)S(1)}, u32[]{:S(2)}, u32[]{:S(2)}) collective-permute-start(bf16[64,1536]{1,0:T(8,128)(2,1)S(1)} %add_convert_fusion), channel_id=1, source_target_pairs={{0,8},{4,12},{8,0},{12,4},{1,9},{5,13},{9,1},{13,5},{2,10},{6,14},... | collective-permute-start | bytes 589832 | tf_op jit(solution)/shard_map/ppermute | solution.py:19
  47.2 1.5 %collective-permute-start.12 = (bf16[128,1536]{1,0:T(8,128)(2,1)S(1)}, bf16[128,1536]{1,0:T(8,128)(2,1)S(1)}, u32[]{:S(2)}, u32[]{:S(2)}) collective-permute-start(bf16[128,1536]{1,0:T(8,128)(2,1)S(1)} %shard_map.93), channel_id=1, source_target_pairs={{0,4},{4,0},{8,12},{12,8},{1,5},{5,1},{9,13},{13,9},{2,6},{6,2},{1... | collective-permute-start | bytes 1179656 | tf_op jit(solution)/shard_map/ppermute | solution.py:19
  48.7 3.4 %collective-permute-done.13 = bf16[64,1536]{1,0:T(8,128)(2,1)S(1)} collective-permute-done((bf16[64,1536]{1,0:T(8,128)(2,1)S(1)}, bf16[64,1536]{1,0:T(8,128)(2,1)S(1)}, u32[]{:S(2)}, u32[]{:S(2)}) %collective-permute-start.13) | collective-permute-done | bytes 196640 | tf_op jit(solution)/shard_map/ppermute | solution.py:19
  52.1 0.6 collective-permute-start.14
  52.8 0.1 copy.10.weights
  52.9 4.5 %collective-permute-done.15.refs_1_ = bf16[64,1536]{1,0:T(8,128)(2,1)S(1)} collective-permute-done((bf16[64,1536]{1,0:T(8,128)(2,1)S(1)}, bf16[64,1536]{1,0:T(8,128)(2,1)S(1)}, u32[]{:S(2)}, u32[]{:S(2)}) %collective-permute-start.15) | collective-permute-done | bytes 196640 | tf_op jit(solution)/shard_map/ppermute | solution.py:19
  57.4 7.5 %collective-permute-done.14.refs_0_ = bf16[64,1536]{1,0:T(8,128)(2,1)S(1)} collective-permute-done((bf16[64,1536]{1,0:T(8,128)(2,1)S(1)}, bf16[64,1536]{1,0:T(8,128)(2,1)S(1)}, u32[]{:S(2)}, u32[]{:S(2)}) %collective-permute-start.14) | collective-permute-done | bytes 196640 | tf_op jit(solution)/shard_map/ppermute | solution.py:19
  65.0 0.7 %collective-permute-done.12.partner = bf16[128,1536]{1,0:T(8,128)(2,1)S(1)} collective-permute-done((bf16[128,1536]{1,0:T(8,128)(2,1)S(1)}, bf16[128,1536]{1,0:T(8,128)(2,1)S(1)}, u32[]{:S(2)}, u32[]{:S(2)}) %collective-permute-start.12) | collective-permute-done | bytes 393248 | tf_op jit(solution)/shard_map/ppermute | solution.py:19
  65.7 1.2 %shard_map.94 = (bf16[128,1536]{1,0:T(8,128)(2,1)}, f32[1,128]{1,0:T(1,128)}) custom-call(bf16[128,1536]{1,0:T(8,128)(2,1)S(1)} %copy-done, bf16[128,1536]{1,0:T(8,128)(2,1)S(1)} %copy-done.1, s32[128,2]{1,0:T(8,128)S(1)} %copy.9.ids, f32[128,2]{1,0:T(8,128)S(1)} %copy.10.weights, f32[128,1536]{1,0:T(8,128)S(1)} %get-tuple-element.11.kept, ...), custom_call_target="tpu_custom_call" | custom-call | flops 3932160 | bytes 3145728 | tf_op jit(solution)/shard_map/pallas_call | solution.py:245
  (31 shorter events, 0.5 us)
Async XLA Ops:
  0.6 4.3 %copy-start.1 = (bf16[128,1536]{1,0:T(8,128)(2,1)S(1)}, bf16[128,1536]{1,0:T(8,128)(2,1)}, u32[]{:S(2)}) copy-start(bf16[128,1536]{1,0:T(8,128)(2,1)} %attn_out.1) | copy-start | bytes 1179652
  0.6 4.3 %copy-start = (bf16[128,1536]{1,0:T(8,128)(2,1)S(1)}, bf16[128,1536]{1,0:T(8,128)(2,1)}, u32[]{:S(2)}) copy-start(bf16[128,1536]{1,0:T(8,128)(2,1)} %layer_in.1) | copy-start | bytes 1179652
  0.6 4.5 %copy-start.4 = (f32[1536]{0:T(1024)S(1)}, f32[1536]{0:T(1024)}, u32[]{:S(2)}) copy-start(f32[1536]{0:T(1024)} %param.9) | copy-start | bytes 18436
  1.9 7.7 %copy-start.3 = (bf16[1,768,384]{2,1,0:T(8,128)(2,1)S(1)}, bf16[1,768,384]{2,1,0:T(8,128)(2,1)}, u32[]{:S(2)}) copy-start(bf16[1,768,384]{2,1,0:T(8,128)(2,1)} %param.13) | copy-start | bytes 1769476
  1.9 19.3 %copy-start.2 = (bf16[1,1536,384]{2,1,0:T(8,128)(2,1)S(1)}, bf16[1,1536,384]{2,1,0:T(8,128)(2,1)}, u32[]{:S(2)}) copy-start(bf16[1,1536,384]{2,1,0:T(8,128)(2,1)} %param.12) | copy-start | bytes 3538948
  1.9 17.2 %collective-permute-start.3 = (bf16[768,384]{1,0:T(8,128)(2,1)S(1)}, bf16[768,384]{1,0:T(8,128)(2,1)S(1)}, u32[]{:S(2)}, u32[]{:S(2)}) collective-permute-start(bf16[768,384]{1,0:T(8,128)(2,1)S(1)} %dynamic-slice_bitcast_fusion), channel_id=1, source_target_pairs={{0,2},{1,3},{2,0},{3,1},{4,6},{5,7},{6,4},{7,5},{8,10},{9,11},{10,... | collective-permute-start | bytes 1769480 | tf_op jit(solution)/shard_map/ppermute | solution.py:19
  5.3 19.0 %collective-permute-start.1 = (bf16[128,1536]{1,0:T(8,128)(2,1)S(1)}, bf16[128,1536]{1,0:T(8,128)(2,1)S(1)}, u32[]{:S(2)}, u32[]{:S(2)}) collective-permute-start(bf16[128,1536]{1,0:T(8,128)(2,1)S(1)} %multiply_convert_fusion.refs_1_), channel_id=1, source_target_pairs={{0,4},{4,0},{8,12},{12,8},{1,5},{5,1},{9,13},{13,9},{2,6},{6,2},{1... | collective-permute-start | bytes 1179656 | tf_op jit(solution)/shard_map/ppermute | solution.py:19
  6.9 19.7 %collective-permute-start = (bf16[128,1536]{1,0:T(8,128)(2,1)S(1)}, bf16[128,1536]{1,0:T(8,128)(2,1)S(1)}, u32[]{:S(2)}, u32[]{:S(2)}) collective-permute-start(bf16[128,1536]{1,0:T(8,128)(2,1)S(1)} %multiply_convert_fusion.refs_1_), channel_id=1, source_target_pairs={{0,8},{4,12},{8,0},{12,4},{1,9},{5,13},{9,1},{13,5},{2,10},{6,14},... | collective-permute-start | bytes 1179656 | tf_op jit(solution)/shard_map/ppermute | solution.py:19
  9.5 21.3 %collective-permute-start.8 = (bf16[768,384]{1,0:T(8,128)(2,1)S(1)}, bf16[768,384]{1,0:T(8,128)(2,1)S(1)}, u32[]{:S(2)}, u32[]{:S(2)}) collective-permute-start(bf16[768,384]{1,0:T(8,128)(2,1)S(1)} %bitcast.8), channel_id=1, source_target_pairs={{0,2},{1,3},{2,0},{3,1},{4,6},{5,7},{6,4},{7,5},{8,10},{9,11},{10,... | collective-permute-start | bytes 1769480 | tf_op jit(solution)/shard_map/ppermute | solution.py:19
  19.0 13.7 %collective-permute-start.4 = (bf16[768,384]{1,0:T(8,128)(2,1)S(1)}, bf16[768,384]{1,0:T(8,128)(2,1)S(1)}, u32[]{:S(2)}, u32[]{:S(2)}) collective-permute-start(bf16[768,384]{1,0:T(8,128)(2,1)S(1)} %collective-permute-done.3.refs_5_.refs_3_), channel_id=1, source_target_pairs={{0,16},{16,0},{1,17},{17,1},{2,18},{18,2},{3,19},{19,3},{4,20},{20... | collective-permute-start | bytes 1769480 | tf_op jit(solution)/shard_map/ppermute | solution.py:19
  21.2 13.8 %collective-permute-start.2 = (bf16[1536,384]{1,0:T(8,128)(2,1)S(1)}, bf16[1536,384]{1,0:T(8,128)(2,1)S(1)}, u32[]{:S(2)}, u32[]{:S(2)}) collective-permute-start(bf16[1536,384]{1,0:T(8,128)(2,1)S(1)} %shard_map.86), channel_id=1, source_target_pairs={{0,1},{1,0},{2,3},{3,2},{4,5},{5,4},{6,7},{7,6},{8,9},{9,8},{10,11... | collective-permute-start | bytes 3538952 | tf_op jit(solution)/shard_map/ppermute | solution.py:19
  26.6 8.4 %collective-permute-start.10 = (bf16[128,1536]{1,0:T(8,128)(2,1)S(1)}, bf16[128,1536]{1,0:T(8,128)(2,1)S(1)}, u32[]{:S(2)}, u32[]{:S(2)}) collective-permute-start(bf16[128,1536]{1,0:T(8,128)(2,1)S(1)} %shard_map.90), channel_id=1, source_target_pairs={{0,4},{4,0},{8,12},{12,8},{1,5},{5,1},{9,13},{13,9},{2,6},{6,2},{1... | collective-permute-start | bytes 1179656 | tf_op jit(solution)/shard_map/ppermute | solution.py:19
  27.1 8.9 %collective-permute-start.7 = (bf16[768,384]{1,0:T(8,128)(2,1)S(1)}, bf16[768,384]{1,0:T(8,128)(2,1)S(1)}, u32[]{:S(2)}, u32[]{:S(2)}) collective-permute-start(bf16[768,384]{1,0:T(8,128)(2,1)S(1)} %bitcast.9), channel_id=1, source_target_pairs={{0,1},{1,0},{2,3},{3,2},{4,5},{5,4},{6,7},{7,6},{8,9},{9,8},{10,11... | collective-permute-start | bytes 1769480 | tf_op jit(solution)/shard_map/ppermute | solution.py:19
  30.9 4.2 %collective-permute-start.5 = (bf16[768,384]{1,0:T(8,128)(2,1)S(1)}, bf16[768,384]{1,0:T(8,128)(2,1)S(1)}, u32[]{:S(2)}, u32[]{:S(2)}) collective-permute-start(bf16[768,384]{1,0:T(8,128)(2,1)S(1)} %collective-permute-done.3.refs_5_.refs_3_), channel_id=1, source_target_pairs={{0,1},{1,0},{2,3},{3,2},{4,5},{5,4},{6,7},{7,6},{8,9},{9,8},{10,11... | collective-permute-start | bytes 1769480 | tf_op jit(solution)/shard_map/ppermute | solution.py:19
  32.7 2.3 %collective-permute-start.6 = (bf16[768,384]{1,0:T(8,128)(2,1)S(1)}, bf16[768,384]{1,0:T(8,128)(2,1)S(1)}, u32[]{:S(2)}, u32[]{:S(2)}) collective-permute-start(bf16[768,384]{1,0:T(8,128)(2,1)S(1)} %collective-permute-done.4.refs_6_.refs_4_), channel_id=1, source_target_pairs={{0,1},{1,0},{2,3},{3,2},{4,5},{5,4},{6,7},{7,6},{8,9},{9,8},{10,11... | collective-permute-start | bytes 1769480 | tf_op jit(solution)/shard_map/ppermute | solution.py:19
  35.0 2.0 %collective-permute-start.9 = (bf16[768,384]{1,0:T(8,128)(2,1)S(1)}, bf16[768,384]{1,0:T(8,128)(2,1)S(1)}, u32[]{:S(2)}, u32[]{:S(2)}) collective-permute-start(bf16[768,384]{1,0:T(8,128)(2,1)S(1)} %shard_map.88), channel_id=1, source_target_pairs={{0,1},{1,0},{2,3},{3,2},{4,5},{5,4},{6,7},{7,6},{8,9},{9,8},{10,11... | collective-permute-start | bytes 1769480 | tf_op jit(solution)/shard_map/ppermute | solution.py:19
  37.6 7.8 %collective-permute-start.11 = (bf16[64,1536]{1,0:T(8,128)(2,1)S(1)}, bf16[64,1536]{1,0:T(8,128)(2,1)S(1)}, u32[]{:S(2)}, u32[]{:S(2)}) collective-permute-start(bf16[64,1536]{1,0:T(8,128)(2,1)S(1)} %get-tuple-element.14), channel_id=1, source_target_pairs={{0,4},{4,0},{8,12},{12,8},{1,5},{5,1},{9,13},{13,9},{2,6},{6,2},{1... | collective-permute-start | bytes 589832 | tf_op jit(solution)/shard_map/ppermute | solution.py:19
  39.4 12.6 %collective-permute-start.13 = (bf16[64,1536]{1,0:T(8,128)(2,1)S(1)}, bf16[64,1536]{1,0:T(8,128)(2,1)S(1)}, u32[]{:S(2)}, u32[]{:S(2)}) collective-permute-start(bf16[64,1536]{1,0:T(8,128)(2,1)S(1)} %get-tuple-element.16), channel_id=1, source_target_pairs={{0,4},{4,0},{8,12},{12,8},{1,5},{5,1},{9,13},{13,9},{2,6},{6,2},{1... | collective-permute-start | bytes 589832 | tf_op jit(solution)/shard_map/ppermute | solution.py:19
  45.4 7.3 %copy-start.5 = (s32[128,2]{0,1:T(2,128)S(1)}, s32[128,2]{0,1:T(2,128)}, u32[]{:S(2)}) copy-start(s32[128,2]{0,1:T(2,128)} %param.10) | copy-start | bytes 3076
  45.4 7.4 %copy-start.6 = (f32[128,2]{0,1:T(2,128)S(1)}, f32[128,2]{0,1:T(2,128)}, u32[]{:S(2)}) copy-start(f32[128,2]{0,1:T(2,128)} %param.11) | copy-start | bytes 3076
  45.5 12.0 %collective-permute-start.15 = (bf16[64,1536]{1,0:T(8,128)(2,1)S(1)}, bf16[64,1536]{1,0:T(8,128)(2,1)S(1)}, u32[]{:S(2)}, u32[]{:S(2)}) collective-permute-start(bf16[64,1536]{1,0:T(8,128)(2,1)S(1)} %add_convert_fusion), channel_id=1, source_target_pairs={{0,8},{4,12},{8,0},{12,4},{1,9},{5,13},{9,1},{13,5},{2,10},{6,14},... | collective-permute-start | bytes 589832 | tf_op jit(solution)/shard_map/ppermute | solution.py:19
  47.2 18.5 %collective-permute-start.12 = (bf16[128,1536]{1,0:T(8,128)(2,1)S(1)}, bf16[128,1536]{1,0:T(8,128)(2,1)S(1)}, u32[]{:S(2)}, u32[]{:S(2)}) collective-permute-start(bf16[128,1536]{1,0:T(8,128)(2,1)S(1)} %shard_map.93), channel_id=1, source_target_pairs={{0,4},{4,0},{8,12},{12,8},{1,5},{5,1},{9,13},{13,9},{2,6},{6,2},{1... | collective-permute-start | bytes 1179656 | tf_op jit(solution)/shard_map/ppermute | solution.py:19
  52.1 12.9 %collective-permute-start.14 = (bf16[64,1536]{1,0:T(8,128)(2,1)S(1)}, bf16[64,1536]{1,0:T(8,128)(2,1)S(1)}, u32[]{:S(2)}, u32[]{:S(2)}) collective-permute-start(bf16[64,1536]{1,0:T(8,128)(2,1)S(1)} %add_convert_fusion.1), channel_id=1, source_target_pairs={{0,8},{4,12},{8,0},{12,4},{1,9},{5,13},{9,1},{13,5},{2,10},{6,14},... | collective-permute-start | bytes 589832 | tf_op jit(solution)/shard_map/ppermute | solution.py:19
